TPU v7x, 32 devices: a whole 2x2x4 slice. The times are simulated.
32 devices in a mesh: cols: 8 (over z, core), rep: 4 (over y, x).
Axes of the slice: x: 2, y: 2, z: 4, core: 2. Of those that a mesh axis runs over, the one named last changes fastest.
Arguments:
- hamiltonian_band: float32 [16, 5, 128, 128], P('cols'), may hold values from -0.25 to 0.25
- margin_factors: float32 [16, 256, 128], P('cols', 'rep'), may hold values from -0.25 to 0.25
- neighbour_mask: int32 [16, 5], P('cols'), may hold values from 0 to 1, as said below
- fermi_level: float32 [1], replicated, may hold values from -0.3 to 0.3
Outputs:
- density: float32 [16, 640, 640], P('cols', 'rep')
Inputs may be any that keep to these rules, and one draw needn't show every extreme that they name: `neighbour_mask`: entry 2 of every row is 1; every row has 3 to 5 ones; some row has 5 ones and some row has exactly 3.
All inputs are finite; a program needn't handle non-finite values.
Results may differ from a plain program's by a relative error of at most 0.0003.
Values sent between devices are 32-bit elements; how exact they have to be, the bound alone decides.
No kernel may reach another device: no remote copies, remote signals or barrier semaphores. Data moves between devices by JAX's collectives and lax.ppermute only.
A program may use at most 64 MiB of HBM per device.

v0:
```python
import functools

import jax
import jax.numpy as jnp
from jax import lax
from jax.experimental import pallas as pl
from jax.experimental.pallas import tpu as pltpu
from jax.sharding import PartitionSpec as P

F32 = jnp.float32
BF16 = jnp.bfloat16


def split(value):
    high = value.astype(BF16)
    return high, (value - high.astype(F32)).astype(BF16)


def dot(left, right):
    return jnp.dot(left, right, preferred_element_type=F32)


def dot3(left, right):
    (left_high, left_low), (right_high, right_low) = left, right
    return dot(left_high, right_high) + (dot(left_high, right_low) + dot(left_low, right_high))


def total(value):
    return jnp.sum(jnp.sum(value, axis=0, keepdims=True), axis=1, keepdims=True)


def eye(rows, columns, first=0):
    row = lax.broadcasted_iota(jnp.int32, (rows, columns), 0) + first
    column = lax.broadcasted_iota(jnp.int32, (rows, columns), 1)
    return jnp.where(row == column, 1.0, 0.0).astype(F32)


def kernel(
    cols, reach, rep_size,
    mask, fermi, place,
    m_left, m_own, m_right, h_left, h_own, h_right,
    out,
    ham, ham_h, ham_l, y_h, y_l, yt_h, yt_l, prod, shift, shift_h, shift_l, sq_h, sq_l,
):
    block = m_own.shape[2]
    depth = m_own.shape[1]
    count = 2 * reach + 1
    width = count * block
    window = cols + 2 * reach

    def margin(w):
        if w < reach:
            return m_left[w]
        if w < reach + cols:
            return m_own[w - reach]
        return m_right[w - reach - cols]

    def band(w, e):
        if w < reach:
            return h_left[w, e]
        if w < reach + cols:
            return h_own[w - reach, e]
        return h_right[w - reach - cols, e]

    def at(index):
        return slice(index * block, (index + 1) * block)

    keep = [[mask[c, a].astype(F32) for a in range(count)] for c in range(cols)]

    trace = [jnp.zeros((1, 1), F32) for _ in range(cols)]
    for w in range(window):
        x = margin(w)
        xt = x.T
        x_sq = total(x * x)
        for c in range(cols):
            a = w - c
            if 0 <= a < count:
                m = keep[c][a]
                high, low = split(x * m)
                y_h[c, :, at(a)] = high
                y_l[c, :, at(a)] = low
                high, low = split(xt * m)
                yt_h[c, at(a), :] = high
                yt_l[c, at(a), :] = low
                trace[c] = trace[c] + x_sq * m

    state = []
    small_eye = eye(depth, depth)
    for c in range(cols):
        gram = dot3((y_h[c], y_l[c]), (yt_h[c], yt_l[c]))
        sum_sq = width + 2.0 * trace[c] + total(gram * gram)
        s0 = 1.0 / (2.0 * jnp.sqrt(sum_sq / width))
        t0 = 1.5 - 0.5 * s0
        u0 = 1.5 - 0.5 * t0 * t0 * s0
        u1 = 0.5 * t0 * (t0 - s0)
        u2 = 0.5 * (0.25 * s0 - t0)
        u3 = 0.125
        e1 = -t0 * u1 - 0.5 * u0
        e2 = -t0 * u2 + 0.5 * u1
        e3 = -t0 * u3 + 0.5 * u2
        e4 = 0.5 * u3
        root = jnp.sqrt(s0)
        kappa = gram * s0
        kappa_s = split(kappa)
        square = dot3(kappa_s, kappa_s)
        cube = dot3(kappa_s, split(square))
        poly = (e1 * small_eye + e2 * kappa + e3 * square + e4 * cube) * (s0 * root)
        poly_s = split(poly)
        p = dot3(poly_s, (y_h[c], y_l[c]))
        pt = dot3((yt_h[c], yt_l[c]), poly_s)
        state.append((t0 * u0 * root, split(p), split(pt)))

    for a in range(window):
        for b in range(a + 1):
            if a - b <= reach:
                value = 0.5 * (band(b, a - b + reach) + band(a, reach - a + b).T)
                high, low = split(value)
                ham[at(a), at(b)] = value
                ham_h[at(a), at(b)] = high
                ham_l[at(a), at(b)] = low
                if a != b:
                    value = value.T
                    high, low = split(value)
            else:
                value = jnp.zeros((block, block), F32)
                high = low = jnp.zeros((block, block), BF16)
                ham[at(a), at(b)] = value
                ham_h[at(a), at(b)] = high
                ham_l[at(a), at(b)] = low
            if a != b:
                ham[at(b), at(a)] = value
                ham_h[at(b), at(a)] = high
                ham_l[at(b), at(a)] = low

    rows = width // rep_size
    first = pl.multiple_of(place[0] * rows, rows)
    big_eye = eye(width, width)
    level = fermi[0]
    scale = []
    for c in range(cols):
        z0, p_s, pt_s = state[c]
        here = slice(c * block, c * block + width)
        mask_col = jnp.concatenate([jnp.full((block, 1), keep[c][a], F32) for a in range(count)], axis=0)
        mask_row = jnp.concatenate([jnp.full((1, block), keep[c][a], F32) for a in range(count)], axis=1)
        side = dot3((ham_h[here, here], ham_l[here, here]), (yt_h[c], yt_l[c])) * mask_col
        core = dot3((y_h[c], y_l[c]), split(side))
        factor = z0 * side + 0.5 * dot3(pt_s, split(core))
        prod[c] = dot3(split(factor), p_s)
        energy = prod[c] + prod[c].T + (ham[here, here] * (z0 * z0 * mask_col)) * mask_row - level * big_eye
        shift[c] = energy
        high, low = split(energy)
        shift_h[c] = high
        shift_l[c] = low
        spread_sq = 4.0 * (total(energy * energy) / width + 1e-05)
        scale.append(1.0 / spread_sq)

    for c in range(cols):
        prod[c] = dot(shift_h[c], shift_l[c])
        square = (dot(shift_h[c], shift_h[c]) + (prod[c] + prod[c].T)) * scale[c]
        high, low = split(square)
        sq_h[c] = high
        sq_l[c] = low

    part_eye = eye(rows, width, first)
    for c in range(cols):
        sq_s = (sq_h[c], sq_l[c])
        x0 = shift[c, pl.ds(first, rows), :] * jnp.sqrt(scale[c])
        x1 = 1.5 * x0 - 0.5 * dot3(split(x0), sq_s)
        y1 = 1.5 * x1 - 0.5 * dot3(split(x1), sq_s)
        y2 = 1.5 * y1 - 0.5 * dot3(split(y1), sq_s)
        y3 = dot3(split(y2), sq_s)
        out[c] = 0.5 * (part_eye - (1.5 * x1 - 0.5 * y3))


def extended(value, reach):
    count = lax.axis_size("cols")
    forward = [(i, (i + 1) % count) for i in range(count)]
    backward = [(target, source) for source, target in forward]
    size = value.shape[0]
    low = lax.ppermute(lax.slice_in_dim(value, size - reach, size, axis=0), "cols", forward)
    high = lax.ppermute(lax.slice_in_dim(value, 0, reach, axis=0), "cols", backward)
    return low, high


def on_device(hamiltonian_band, margin_factors, neighbour_mask, fermi_level):
    cols, count, block, _ = hamiltonian_band.shape
    reach = (count - 1) // 2
    width = count * block
    rep_size = lax.axis_size("rep")
    rows = width // rep_size
    h_left, h_right = extended(hamiltonian_band, reach)
    factors = lax.all_gather(margin_factors, "rep", axis=1, tiled=True)
    m_left, m_right = extended(factors, reach)
    place = lax.axis_index("rep").astype(jnp.int32).reshape(1)
    depth = factors.shape[1]
    window = (cols + 2 * reach) * block
    smem = pl.BlockSpec(memory_space=pltpu.SMEM)
    vmem = pl.BlockSpec(memory_space=pltpu.VMEM)
    return pl.pallas_call(
        functools.partial(kernel, cols, reach, rep_size),
        out_shape=jax.ShapeDtypeStruct((cols, rows, width), F32),
        in_specs=[smem] * 3 + [vmem] * 6,
        out_specs=vmem,
        scratch_shapes=[
            pltpu.VMEM((window, window), F32),
            pltpu.VMEM((window, window), BF16),
            pltpu.VMEM((window, window), BF16),
            pltpu.VMEM((cols, depth, width), BF16),
            pltpu.VMEM((cols, depth, width), BF16),
            pltpu.VMEM((cols, width, depth), BF16),
            pltpu.VMEM((cols, width, depth), BF16),
            pltpu.VMEM((cols, width, width), F32),
            pltpu.VMEM((cols, width, width), F32),
            pltpu.VMEM((cols, width, width), BF16),
            pltpu.VMEM((cols, width, width), BF16),
            pltpu.VMEM((cols, width, width), BF16),
            pltpu.VMEM((cols, width, width), BF16),
        ],
        compiler_params=pltpu.CompilerParams(vmem_limit_bytes=48 * 2**20),
    )(neighbour_mask, fermi_level, place, m_left, factors, m_right, h_left, hamiltonian_band, h_right)


def solution(mesh):
    in_specs = (P("cols", None, None, None), P("cols", "rep", None), P("cols", None), P())
    out_specs = P("cols", "rep", None)
    return jax.shard_map(
        on_device, mesh=mesh, in_specs=in_specs, out_specs=out_specs, check_vma=False
    )
```

profile of v0, /device:TPU:0, one launch (start us, length us, event | category | flops | bytes accessed | tf_op | source)
XLA Modules:
  0.0 49.1 jit_solution(15296977524377419711)
XLA Ops:
  0.0 0.5 collective-permute-start.2
  0.5 4.0 %collective-permute-start.3 = (f32[2,5,128,128]{3,2,1,0:T(8,128)}, f32[2,5,128,128]{3,2,1,0:T(8,128)S(1)}, u32[]{:S(2)}, u32[]{:S(2)}) collective-permute-start(f32[2,5,128,128]{3,2,1,0:T(8,128)} %h_own.1), channel_id=1, source_target_pairs={{4,0},{8,4},{12,8},{16,12},{20,16},{24,20},{28,24},{0,28},{5,1},{9... | collective-permute-start | bytes 1966088 | tf_op jit(solution)/shard_map/ppermute | solution.py:181
  4.5 10.1 %all_gather.3.m_own = f32[2,256,128]{2,1,0:T(8,128)S(1)} all-gather(f32[2,64,128]{2,1,0:T(8,128)} %param.5), channel_id=1, replica_groups=mesh['cols'=8,'rep'=4] {'rep'}, dimensions={1}, use_global_device_ids=true | all-gather | bytes 327680 | tf_op jit(solution)/shard_map/all_gather | solution.py:192
  14.6 0.0 collective-permute-start.1
  14.6 0.5 %collective-permute-start = (f32[2,256,128]{2,1,0:T(8,128)S(1)}, f32[2,256,128]{2,1,0:T(8,128)S(1)}, u32[]{:S(2)}, u32[]{:S(2)}) collective-permute-start(f32[2,256,128]{2,1,0:T(8,128)S(1)} %all_gather.3.m_own), channel_id=1, source_target_pairs={{0,4},{4,8},{8,12},{12,16},{16,20},{20,24},{24,28},{28,0},{1,5},{5... | collective-permute-start | bytes 786440 | tf_op jit(solution)/shard_map/ppermute | solution.py:180
  15.8 0.0 copy-start.1
  15.8 7.7 %collective-permute-done.1.m_right = f32[2,256,128]{2,1,0:T(8,128)S(1)} collective-permute-done((f32[2,256,128]{2,1,0:T(8,128)S(1)}, f32[2,256,128]{2,1,0:T(8,128)S(1)}, u32[]{:S(2)}, u32[]{:S(2)}) %collective-permute-start.1) | collective-permute-done | bytes 262176 | tf_op jit(solution)/shard_map/ppermute | solution.py:181
  23.5 1.7 %collective-permute-done.m_left = f32[2,256,128]{2,1,0:T(8,128)S(1)} collective-permute-done((f32[2,256,128]{2,1,0:T(8,128)S(1)}, f32[2,256,128]{2,1,0:T(8,128)S(1)}, u32[]{:S(2)}, u32[]{:S(2)}) %collective-permute-start) | collective-permute-done | bytes 262176 | tf_op jit(solution)/shard_map/ppermute | solution.py:180
  25.1 0.0 collective-permute-done.2.h_left
  25.1 0.0 collective-permute-done.3.h_right
  25.1 0.0 copy-done.1
  25.1 0.0 copy-start
  25.2 1.1 %copy-done = f32[2,5,128,128]{3,2,1,0:T(8,128)S(1)} copy-done((f32[2,5,128,128]{3,2,1,0:T(8,128)S(1)}, f32[2,5,128,128]{3,2,1,0:T(8,128)}, u32[]{:S(2)}) %copy-start) | copy-done | bytes 655384
  26.2 22.8 %shard_map.46 = f32[2,160,640]{2,1,0:T(8,128)} custom-call(s32[2,5]{1,0:T(2,128)S(1)} %copy-done.1, f32[1]{0:T(128)S(6)} %copy.5.fermi, s32[1]{0:T(128)} %bitcast.place, f32[2,256,128]{2,1,0:T(8,128)S(1)} %collective-permute-done.m_left, f32[2,256,128]{2,1,0:T(8,128)S(1)} %all_gather.3.m_own, f32[2,256,128]{2,1,0:T(8,128)S(1)} %collective-permute-done.1.m_right, ...), custom_call_target="tpu_custom_call" | custom-call | tf_op jit(solution)/shard_map/pallas_call | solution.py:199
Async XLA Ops:
  0.0 25.1 %collective-permute-start.2 = (f32[2,5,128,128]{3,2,1,0:T(8,128)}, f32[2,5,128,128]{3,2,1,0:T(8,128)S(1)}, u32[]{:S(2)}, u32[]{:S(2)}) collective-permute-start(f32[2,5,128,128]{3,2,1,0:T(8,128)} %h_own.1), channel_id=1, source_target_pairs={{0,4},{4,8},{8,12},{12,16},{16,20},{20,24},{24,28},{28,0},{1,5},{5... | collective-permute-start | bytes 1966088 | tf_op jit(solution)/shard_map/ppermute | solution.py:180
  0.5 24.7 %collective-permute-start.3 = (f32[2,5,128,128]{3,2,1,0:T(8,128)}, f32[2,5,128,128]{3,2,1,0:T(8,128)S(1)}, u32[]{:S(2)}, u32[]{:S(2)}) collective-permute-start(f32[2,5,128,128]{3,2,1,0:T(8,128)} %h_own.1), channel_id=1, source_target_pairs={{4,0},{8,4},{12,8},{16,12},{20,16},{24,20},{28,24},{0,28},{5,1},{9... | collective-permute-start | bytes 1966088 | tf_op jit(solution)/shard_map/ppermute | solution.py:181
  14.6 8.8 %collective-permute-start.1 = (f32[2,256,128]{2,1,0:T(8,128)S(1)}, f32[2,256,128]{2,1,0:T(8,128)S(1)}, u32[]{:S(2)}, u32[]{:S(2)}) collective-permute-start(f32[2,256,128]{2,1,0:T(8,128)S(1)} %all_gather.3.m_own), channel_id=1, source_target_pairs={{4,0},{8,4},{12,8},{16,12},{20,16},{24,20},{28,24},{0,28},{5,1},{9... | collective-permute-start | bytes 786440 | tf_op jit(solution)/shard_map/ppermute | solution.py:181
  14.6 10.5 %collective-permute-start = (f32[2,256,128]{2,1,0:T(8,128)S(1)}, f32[2,256,128]{2,1,0:T(8,128)S(1)}, u32[]{:S(2)}, u32[]{:S(2)}) collective-permute-start(f32[2,256,128]{2,1,0:T(8,128)S(1)} %all_gather.3.m_own), channel_id=1, source_target_pairs={{0,4},{4,8},{8,12},{12,16},{16,20},{20,24},{24,28},{28,0},{1,5},{5... | collective-permute-start | bytes 786440 | tf_op jit(solution)/shard_map/ppermute | solution.py:180
  15.8 9.4 %copy-start.1 = (s32[2,5]{1,0:T(2,128)S(1)}, s32[2,5]{1,0:T(2,128)}, u32[]{:S(2)}) copy-start(s32[2,5]{1,0:T(2,128)} %mask.1) | copy-start | bytes 124
  25.1 1.1 %copy-start = (f32[2,5,128,128]{3,2,1,0:T(8,128)S(1)}, f32[2,5,128,128]{3,2,1,0:T(8,128)}, u32[]{:S(2)}) copy-start(f32[2,5,128,128]{3,2,1,0:T(8,128)} %h_own.1) | copy-start | bytes 1966084
where the time goes:
time: 49.3 us; the launch traced here: 49.1 us
  Pallas kernels  22.8 us (46%)
  blocking collectives  10.1 us (20%)
  waiting for transfers between devices  9.36 us (19%)
  starting transfers between devices  5 us (10%)
  local copies, waits for them, and re-layouts  1.09 us (2%)
  between operations  0.68 us (1%)
    pallas_call x1, Pallas kernels, on_device(): pl.pallas_call(functools.partial(kernel, cols, reach, rep_size), out_shap...  22.8 us
    all_gather x1, blocking collectives, on_device(): factors = lax.all_gather(margin_factors, 'rep', axis=1, tiled=True)  10.1 us
    ppermute x2, waiting for transfers between devices, extended(): lax.ppermute(lax.slice_in_dim(value, 0, reach, axis=0), 'cols', backward)  7.67 us
    ppermute x2, starting transfers between devices, extended(): lax.ppermute(lax.slice_in_dim(value, 0, reach, axis=0), 'cols', backward)  4.04 us
    ppermute x2, waiting for transfers between devices, extended(): lax.ppermute(lax.slice_in_dim(value, size - reach, size, axis=0), 'cols',...  1.69 us
    unnamed x4, local copies, waits for them, and re-layouts  1.09 us
  transfers between devices with their start and end apart: 4, of which 2 were waited for; matrix products, arithmetic and copies ran while one was open for 0% of the time, Pallas kernels for 0%

commit v1 on v0

v1 whole, which is shorter than its diff:
```python
import functools

import jax
import jax.numpy as jnp
from jax import lax
from jax.experimental import pallas as pl
from jax.experimental.pallas import tpu as pltpu
from jax.sharding import PartitionSpec as P

F32 = jnp.float32
BF16 = jnp.bfloat16
PACKED = 16


def split(value):
    high = value.astype(BF16)
    return high, (value - high.astype(F32)).astype(BF16)


def dot(left, right):
    return jnp.dot(left, right, preferred_element_type=F32)


def dot3(left, right):
    (left_high, left_low), (right_high, right_low) = left, right
    return dot(
        jnp.concatenate([left_high, left_low, left_high], axis=1),
        jnp.concatenate([right_high, right_high, right_low], axis=0),
    )


def total(value):
    return jnp.sum(jnp.sum(value, axis=0, keepdims=True), axis=1, keepdims=True)


def eye(rows, columns, first=0):
    row = lax.broadcasted_iota(jnp.int32, (rows, columns), 0) + first
    column = lax.broadcasted_iota(jnp.int32, (rows, columns), 1)
    return jnp.where(row == column, 1.0, 0.0).astype(F32)


def kernel(
    cols, reach, rep_size,
    mask, fermi, place,
    m_left, m_own, m_right, h_left, h_own, h_right,
    out,
    ham, ham_h, ham_l, y_h, y_l, yt_h, yt_l, prod, shift_h, shift_l, sq_h, sq_l, side_h, side_l, whole,
):
    block = m_own.shape[2]
    depth = m_own.shape[1]
    count = 2 * reach + 1
    width = count * block
    window = cols + 2 * reach
    rows = width // rep_size
    columns = range(cols)

    def margin(w):
        if w < reach:
            return m_left[w]
        if w < reach + cols:
            return m_own[w - reach]
        return m_right[w - reach - cols]

    def band(w, e):
        if w < reach:
            return h_left[w, e]
        if w < reach + cols:
            return h_own[w - reach, e]
        return h_right[w - reach - cols, e]

    def at(index):
        return slice(index * block, (index + 1) * block)

    keep = [[mask[c, a].astype(F32) for a in range(count)] for c in columns]

    trace = [jnp.zeros((1, 1), F32) for _ in columns]
    for w in range(window):
        x = margin(w)
        xt = x.T
        x_sq = total(x * x)
        for c in columns:
            a = w - c
            if 0 <= a < count:
                m = keep[c][a]
                y_h[c, :, at(a)], y_l[c, :, at(a)] = split(x * m)
                yt_h[c, at(a), :], yt_l[c, at(a), :] = split(xt * m)
                trace[c] = trace[c] + x_sq * m

    for a in range(window):
        for b in range(a + 1):
            if a - b <= reach:
                value = 0.5 * (band(b, a - b + reach) + band(a, reach - a + b).T)
                ham[at(a), at(b)] = value
                ham_h[at(a), at(b)], ham_l[at(a), at(b)] = split(value)
                if a != b:
                    value = value.T
                    ham[at(b), at(a)] = value
                    ham_h[at(b), at(a)], ham_l[at(b), at(a)] = split(value)
            else:
                none = jnp.zeros((block, block), BF16)
                for i, j in ((a, b), (b, a)):
                    ham_h[at(i), at(j)] = none
                    ham_l[at(i), at(j)] = none

    small_eye = eye(depth, depth)
    gram = [dot3((y_h[c], y_l[c]), (yt_h[c], yt_l[c])) for c in columns]
    coef = []
    kappa = []
    for c in columns:
        sum_sq = width + 2.0 * trace[c] + total(gram[c] * gram[c])
        s0 = 1.0 / (2.0 * jnp.sqrt(sum_sq / width))
        t0 = 1.5 - 0.5 * s0
        u0 = 1.5 - 0.5 * t0 * t0 * s0
        u1 = 0.5 * t0 * (t0 - s0)
        u2 = 0.5 * (0.25 * s0 - t0)
        u3 = 0.125
        root = jnp.sqrt(s0)
        factor = s0 * root
        e1 = (-t0 * u1 - 0.5 * u0) * factor
        e2 = (-t0 * u2 + 0.5 * u1) * factor
        e3 = (-t0 * u3 + 0.5 * u2) * factor
        e4 = 0.5 * u3 * factor
        coef.append((t0 * u0 * root, e1, e2, e3, e4))
        kappa.append(gram[c] * s0)
    kappa_s = [split(kappa[c]) for c in columns]
    square = [dot3(kappa_s[c], kappa_s[c]) for c in columns]
    cube = [dot3(kappa_s[c], split(square[c])) for c in columns]
    poly = []
    for c in columns:
        _, e1, e2, e3, e4 = coef[c]
        poly.append(e1 * small_eye + e2 * kappa[c] + e3 * square[c] + e4 * cube[c])
    poly_s = [split(poly[c]) for c in columns]

    core = []
    for c in columns:
        here = slice(c * block, c * block + width)
        side = dot3((ham_h[here, here], ham_l[here, here]), (yt_h[c], yt_l[c]))
        for a in range(count):
            side_h[c, at(a), :], side_l[c, at(a), :] = split(side[at(a)] * keep[c][a])
    for c in columns:
        core.append(dot3((y_h[c], y_l[c]), (side_h[c], side_l[c])))

    core = [dot3(poly_s[c], split(core[c])) for c in columns]
    core = [dot3(split(core[c]), poly_s[c]) for c in columns]
    factor = []
    for c in columns:
        left = tuple(
            jnp.concatenate(pair, axis=1) for pair in ((side_h[c], yt_h[c]), (side_l[c], yt_l[c]))
        )
        right = split(jnp.concatenate([coef[c][0] * poly[c], 0.5 * core[c]], axis=0))
        factor.append(split(dot3(left, right)))
    for c in columns:
        prod[c] = dot3(factor[c], (y_h[c], y_l[c]))

    level = fermi[0] * eye(block, block)
    scale = []
    for c in columns:
        z0_sq = coef[c][0] * coef[c][0]
        sum_sq = jnp.zeros((block, block), F32)
        for a in range(count):
            for b in range(count):
                value = prod[c, at(a), at(b)] + prod[c, at(b), at(a)].T
                if abs(a - b) <= reach:
                    value = value + ham[at(c + a), at(c + b)] * (z0_sq * (keep[c][a] * keep[c][b]))
                if a == b:
                    value = value - level
                sum_sq = sum_sq + value * value
                if rows % PACKED:
                    whole[c, at(a), at(b)] = value
                high = value.astype(BF16)
                shift_h[c, at(a), at(b)] = high
                shift_l[c, at(a), at(b)] = (2.0 * (value - high.astype(F32))).astype(BF16)
        scale.append(1.0 / (4.0 * (total(sum_sq) / width + 1e-05)))

    for c in columns:
        high = shift_h[c]
        prod[c] = dot(
            jnp.concatenate([high, high], axis=1), jnp.concatenate([high, shift_l[c]], axis=0)
        )

    for c in columns:
        half = 0.5 * scale[c]
        for a in range(count):
            for b in range(count):
                value = (prod[c, at(a), at(b)] + prod[c, at(b), at(a)].T) * half
                sq_h[c, at(a), at(b)], sq_l[c, at(a), at(b)] = split(value)

    first = pl.multiple_of(place[0] * rows, rows)
    part_eye = eye(rows, width, first)
    own = pl.ds(first, rows)
    sq_s = [(sq_h[c], sq_l[c]) for c in columns]
    if rows % PACKED:
        x0 = [whole[c, own, :] for c in columns]
    else:
        x0 = [shift_h[c, own, :].astype(F32) + 0.5 * shift_l[c, own, :].astype(F32) for c in columns]
    x0 = [x0[c] * jnp.sqrt(scale[c]) for c in columns]
    x1 = [1.5 * x0[c] - 0.5 * dot3(split(x0[c]), sq_s[c]) for c in columns]
    y1 = [1.5 * x1[c] - 0.5 * dot3(split(x1[c]), sq_s[c]) for c in columns]
    y2 = [1.5 * y1[c] - 0.5 * dot3(split(y1[c]), sq_s[c]) for c in columns]
    for c in columns:
        y3 = dot3(split(y2[c]), sq_s[c])
        out[c] = 0.5 * (part_eye - (1.5 * x1[c] - 0.5 * y3))


def call(neighbour_mask, fermi_level, place, m_left, factors, m_right, h_left, hamiltonian_band, h_right, rep_size):
    cols, count, block, _ = hamiltonian_band.shape
    reach = (count - 1) // 2
    width = count * block
    rows = width // rep_size
    depth = factors.shape[1]
    window = (cols + 2 * reach) * block
    smem = pl.BlockSpec(memory_space=pltpu.SMEM)
    vmem = pl.BlockSpec(memory_space=pltpu.VMEM)
    return pl.pallas_call(
        functools.partial(kernel, cols, reach, rep_size),
        out_shape=jax.ShapeDtypeStruct((cols, rows, width), F32),
        in_specs=[smem] * 3 + [vmem] * 6,
        out_specs=vmem,
        scratch_shapes=[
            pltpu.VMEM((window, window), F32),
            pltpu.VMEM((window, window), BF16),
            pltpu.VMEM((window, window), BF16),
            pltpu.VMEM((cols, depth, width), BF16),
            pltpu.VMEM((cols, depth, width), BF16),
            pltpu.VMEM((cols, width, depth), BF16),
            pltpu.VMEM((cols, width, depth), BF16),
            pltpu.VMEM((cols, width, width), F32),
            pltpu.VMEM((cols, width, width), BF16),
            pltpu.VMEM((cols, width, width), BF16),
            pltpu.VMEM((cols, width, width), BF16),
            pltpu.VMEM((cols, width, width), BF16),
            pltpu.VMEM((cols, width, depth), BF16),
            pltpu.VMEM((cols, width, depth), BF16),
            pltpu.VMEM((cols, width, width) if rows % PACKED else (1, 8, 128), F32),
        ],
        compiler_params=pltpu.CompilerParams(vmem_limit_bytes=48 * 2**20),
    )(neighbour_mask, fermi_level, place, m_left, factors, m_right, h_left, hamiltonian_band, h_right)


def extended(value, reach):
    count = lax.axis_size("cols")
    forward = [(i, (i + 1) % count) for i in range(count)]
    backward = [(target, source) for source, target in forward]
    size = value.shape[0]
    low = lax.ppermute(lax.slice_in_dim(value, size - reach, size, axis=0), "cols", forward)
    high = lax.ppermute(lax.slice_in_dim(value, 0, reach, axis=0), "cols", backward)
    return low, high


def on_device(hamiltonian_band, margin_factors, neighbour_mask, fermi_level):
    cols, count, block, _ = hamiltonian_band.shape
    reach = (count - 1) // 2
    rep_size = lax.axis_size("rep")
    h_left, h_right = extended(hamiltonian_band, reach)
    factors = lax.all_gather(margin_factors, "rep", axis=1, tiled=True)
    m_left, m_right = extended(factors, reach)
    place = lax.axis_index("rep").astype(jnp.int32).reshape(1)
    return call(neighbour_mask, fermi_level, place, m_left, factors, m_right, h_left, hamiltonian_band, h_right, rep_size)


def solution(mesh):
    in_specs = (P("cols", None, None, None), P("cols", "rep", None), P("cols", None), P())
    out_specs = P("cols", "rep", None)
    return jax.shard_map(
        on_device, mesh=mesh, in_specs=in_specs, out_specs=out_specs, check_vma=False
    )
```

time: 49.3 us -> 42.1 us (0.85)
  Pallas kernels: 22.8 us -> 15.6 us
    pallas_call x1, Pallas kernels: 22.8 us -> 15.6 us  [call(): pl.pallas_call(functools.partial(kernel, cols, reach, rep_size), out_shap...]
where the time goes in v1:
time: 42.1 us; the launch traced here: 41.8 us
  Pallas kernels  15.6 us (37%)
  blocking collectives  10.1 us (24%)
  waiting for transfers between devices  9.36 us (22%)
  starting transfers between devices  5 us (12%)
  local copies, waits for them, and re-layouts  1.09 us (3%)
  between operations  0.68 us (2%)
    pallas_call x1, Pallas kernels, call(): pl.pallas_call(functools.partial(kernel, cols, reach, rep_size), out_shap...  15.6 us
    all_gather x1, blocking collectives, on_device(): factors = lax.all_gather(margin_factors, 'rep', axis=1, tiled=True)  10.1 us
    ppermute x2, waiting for transfers between devices, extended(): lax.ppermute(lax.slice_in_dim(value, 0, reach, axis=0), 'cols', backward)  7.67 us
    ppermute x2, starting transfers between devices, extended(): lax.ppermute(lax.slice_in_dim(value, 0, reach, axis=0), 'cols', backward)  4.04 us
    ppermute x2, waiting for transfers between devices, extended(): lax.ppermute(lax.slice_in_dim(value, size - reach, size, axis=0), 'cols',...  1.69 us
    unnamed x4, local copies, waits for them, and re-layouts  1.09 us
    ppermute x2, starting transfers between devices, extended(): lax.ppermute(lax.slice_in_dim(value, size - reach, size, axis=0), 'cols',...  0.96 us
  transfers between devices with their start and end apart: 4, of which 2 were waited for; matrix products, arithmetic and copies ran while one was open for 0% of the time, Pallas kernels for 0%

profile of v1, /device:TPU:0, one launch (start us, length us, event | category | flops | bytes accessed | tf_op | source)
XLA Modules:
  0.0 41.8 jit_solution(8849146538908471267)
XLA Ops:
  0.0 0.5 %collective-permute-start.2 = (f32[2,5,128,128]{3,2,1,0:T(8,128)}, f32[2,5,128,128]{3,2,1,0:T(8,128)S(1)}, u32[]{:S(2)}, u32[]{:S(2)}) collective-permute-start(f32[2,5,128,128]{3,2,1,0:T(8,128)} %h_own.1), channel_id=1, source_target_pairs={{0,4},{4,8},{8,12},{12,16},{16,20},{20,24},{24,28},{28,0},{1,5},{5... | collective-permute-start | bytes 1966088 | tf_op jit(solution)/shard_map/ppermute | solution.py:245
  0.5 4.0 %collective-permute-start.3 = (f32[2,5,128,128]{3,2,1,0:T(8,128)}, f32[2,5,128,128]{3,2,1,0:T(8,128)S(1)}, u32[]{:S(2)}, u32[]{:S(2)}) collective-permute-start(f32[2,5,128,128]{3,2,1,0:T(8,128)} %h_own.1), channel_id=1, source_target_pairs={{4,0},{8,4},{12,8},{16,12},{20,16},{24,20},{28,24},{0,28},{5,1},{9... | collective-permute-start | bytes 1966088 | tf_op jit(solution)/shard_map/ppermute | solution.py:246
  4.5 10.1 %all_gather.3.m_own = f32[2,256,128]{2,1,0:T(8,128)S(1)} all-gather(f32[2,64,128]{2,1,0:T(8,128)} %param.5), channel_id=1, replica_groups=mesh['cols'=8,'rep'=4] {'rep'}, dimensions={1}, use_global_device_ids=true | all-gather | bytes 327680 | tf_op jit(solution)/shard_map/all_gather | solution.py:255
  14.6 0.0 collective-permute-start.1
  14.6 0.5 %collective-permute-start = (f32[2,256,128]{2,1,0:T(8,128)S(1)}, f32[2,256,128]{2,1,0:T(8,128)S(1)}, u32[]{:S(2)}, u32[]{:S(2)}) collective-permute-start(f32[2,256,128]{2,1,0:T(8,128)S(1)} %all_gather.3.m_own), channel_id=1, source_target_pairs={{0,4},{4,8},{8,12},{12,16},{16,20},{20,24},{24,28},{28,0},{1,5},{5... | collective-permute-start | bytes 786440 | tf_op jit(solution)/shard_map/ppermute | solution.py:245
  15.8 0.0 copy-start.1
  15.8 7.7 %collective-permute-done.1.m_right = f32[2,256,128]{2,1,0:T(8,128)S(1)} collective-permute-done((f32[2,256,128]{2,1,0:T(8,128)S(1)}, f32[2,256,128]{2,1,0:T(8,128)S(1)}, u32[]{:S(2)}, u32[]{:S(2)}) %collective-permute-start.1) | collective-permute-done | bytes 262176 | tf_op jit(solution)/shard_map/ppermute | solution.py:246
  23.5 1.7 %collective-permute-done.m_left = f32[2,256,128]{2,1,0:T(8,128)S(1)} collective-permute-done((f32[2,256,128]{2,1,0:T(8,128)S(1)}, f32[2,256,128]{2,1,0:T(8,128)S(1)}, u32[]{:S(2)}, u32[]{:S(2)}) %collective-permute-start) | collective-permute-done | bytes 262176 | tf_op jit(solution)/shard_map/ppermute | solution.py:245
  25.1 0.0 collective-permute-done.2.h_left
  25.1 0.0 collective-permute-done.3.h_right
  25.1 0.0 copy-done.1
  25.1 0.0 copy-start
  25.2 1.1 %copy-done = f32[2,5,128,128]{3,2,1,0:T(8,128)S(1)} copy-done((f32[2,5,128,128]{3,2,1,0:T(8,128)S(1)}, f32[2,5,128,128]{3,2,1,0:T(8,128)}, u32[]{:S(2)}) %copy-start) | copy-done | bytes 655384
  26.2 15.6 %shard_map.46 = f32[2,160,640]{2,1,0:T(8,128)} custom-call(s32[2,5]{1,0:T(2,128)S(1)} %copy-done.1, f32[1]{0:T(128)S(6)} %copy.5.fermi, s32[1]{0:T(128)} %bitcast.place, f32[2,256,128]{2,1,0:T(8,128)S(1)} %collective-permute-done.m_left, f32[2,256,128]{2,1,0:T(8,128)S(1)} %all_gather.3.m_own, f32[2,256,128]{2,1,0:T(8,128)S(1)} %collective-permute-done.1.m_right, ...), custom_call_target="tpu_custom_call" | custom-call | tf_op jit(solution)/shard_map/pallas_call | solution.py:214
Async XLA Ops:
  0.0 25.1 %collective-permute-start.2 = (f32[2,5,128,128]{3,2,1,0:T(8,128)}, f32[2,5,128,128]{3,2,1,0:T(8,128)S(1)}, u32[]{:S(2)}, u32[]{:S(2)}) collective-permute-start(f32[2,5,128,128]{3,2,1,0:T(8,128)} %h_own.1), channel_id=1, source_target_pairs={{0,4},{4,8},{8,12},{12,16},{16,20},{20,24},{24,28},{28,0},{1,5},{5... | collective-permute-start | bytes 1966088 | tf_op jit(solution)/shard_map/ppermute | solution.py:245
  0.5 24.7 %collective-permute-start.3 = (f32[2,5,128,128]{3,2,1,0:T(8,128)}, f32[2,5,128,128]{3,2,1,0:T(8,128)S(1)}, u32[]{:S(2)}, u32[]{:S(2)}) collective-permute-start(f32[2,5,128,128]{3,2,1,0:T(8,128)} %h_own.1), channel_id=1, source_target_pairs={{4,0},{8,4},{12,8},{16,12},{20,16},{24,20},{28,24},{0,28},{5,1},{9... | collective-permute-start | bytes 1966088 | tf_op jit(solution)/shard_map/ppermute | solution.py:246
  14.6 8.8 %collective-permute-start.1 = (f32[2,256,128]{2,1,0:T(8,128)S(1)}, f32[2,256,128]{2,1,0:T(8,128)S(1)}, u32[]{:S(2)}, u32[]{:S(2)}) collective-permute-start(f32[2,256,128]{2,1,0:T(8,128)S(1)} %all_gather.3.m_own), channel_id=1, source_target_pairs={{4,0},{8,4},{12,8},{16,12},{20,16},{24,20},{28,24},{0,28},{5,1},{9... | collective-permute-start | bytes 786440 | tf_op jit(solution)/shard_map/ppermute | solution.py:246
  14.6 10.5 %collective-permute-start = (f32[2,256,128]{2,1,0:T(8,128)S(1)}, f32[2,256,128]{2,1,0:T(8,128)S(1)}, u32[]{:S(2)}, u32[]{:S(2)}) collective-permute-start(f32[2,256,128]{2,1,0:T(8,128)S(1)} %all_gather.3.m_own), channel_id=1, source_target_pairs={{0,4},{4,8},{8,12},{12,16},{16,20},{20,24},{24,28},{28,0},{1,5},{5... | collective-permute-start | bytes 786440 | tf_op jit(solution)/shard_map/ppermute | solution.py:245
  15.8 9.4 %copy-start.1 = (s32[2,5]{1,0:T(2,128)S(1)}, s32[2,5]{1,0:T(2,128)}, u32[]{:S(2)}) copy-start(s32[2,5]{1,0:T(2,128)} %mask.1) | copy-start | bytes 124
  25.1 1.1 %copy-start = (f32[2,5,128,128]{3,2,1,0:T(8,128)S(1)}, f32[2,5,128,128]{3,2,1,0:T(8,128)}, u32[]{:S(2)}) copy-start(f32[2,5,128,128]{3,2,1,0:T(8,128)} %h_own.1) | copy-start | bytes 1966084

commit v2 on v1

v2 whole, which is shorter than its diff:
```python
import functools

import jax
import jax.numpy as jnp
from jax import lax
from jax.experimental import pallas as pl
from jax.experimental.pallas import tpu as pltpu
from jax.sharding import PartitionSpec as P

F32 = jnp.float32
BF16 = jnp.bfloat16
PACKED = 16
TILE = 8


def split(value):
    high = value.astype(BF16)
    return high, (value - high.astype(F32)).astype(BF16)


def dot(left, right):
    return jnp.dot(left, right, preferred_element_type=F32)


def dot3(left, right):
    (left_high, left_low), (right_high, right_low) = left, right
    return dot(
        jnp.concatenate([left_high, left_low, left_high], axis=1),
        jnp.concatenate([right_high, right_high, right_low], axis=0),
    )


def total(value):
    return jnp.sum(jnp.sum(value, axis=0, keepdims=True), axis=1, keepdims=True)


def eye(rows, columns, first=0):
    row = lax.broadcasted_iota(jnp.int32, (rows, columns), 0) + first
    column = lax.broadcasted_iota(jnp.int32, (rows, columns), 1)
    return jnp.where(row == column, 1.0, 0.0).astype(F32)


def upper(block):
    row = lax.broadcasted_iota(jnp.int32, (block, block), 0)
    return row <= lax.broadcasted_iota(jnp.int32, (block, block), 1)


def crossing(reach):
    return [(i, j) for j in range(reach) for i in range(reach) if reach + j - i <= reach]


def edge_kernel(reach, even, band, far, near, kept):
    block = band.shape[2]
    cross = crossing(reach)
    first = 0.5 * (band[0, reach] + band[0, reach].T)
    second = 0.5 * (band[1, reach] + band[1, reach].T)
    below = 0.5 * (band[0, reach + 1] + band[1, reach - 1].T)
    mixed = jnp.where(upper(block), first, second)
    diagonal = jnp.sum(second * eye(block, block), axis=0, keepdims=True)
    for out in (far, near):
        out[0:block] = mixed
        out[block : 2 * block] = below
        out[(2 + len(cross)) * block :] = jnp.broadcast_to(diagonal, (TILE, block))
    kept[0] = first
    kept[1] = below
    kept[2] = second
    is_even = even[0] == 1
    for index, (i, j) in enumerate(cross):
        to_left = band[j, i - j]
        to_right = band[i, 2 * reach + j - i]
        here = slice((2 + index) * block, (3 + index) * block)
        far[here] = jnp.where(is_even, to_left, to_right)
        near[here] = jnp.where(is_even, to_right, to_left)
        kept[3 + index] = to_left
        kept[3 + len(cross) + index] = to_right


def root_kernel(cols, reach, rep_size, even, mask, *refs):
    groups = refs[:rep_size]
    nears = refs[rep_size : 2 * rep_size]
    y_h, y_l, yt_h, yt_l, poly, unit = refs[2 * rep_size :]
    piece, block = groups[0].shape[1:]
    count = 2 * reach + 1
    window = cols + 2 * reach
    width = count * block
    columns = range(cols)
    is_even = even[0] == 1

    def margin(w):
        parts = []
        for group, near in zip(groups, nears):
            if reach <= w < reach + cols:
                parts.append(group[w - reach])
            elif w < reach:
                parts.append(jnp.where(is_even, group[cols + w], near[w]))
            else:
                parts.append(jnp.where(is_even, near[w - reach - cols], group[w - reach]))
        return jnp.concatenate(parts, axis=0)

    def at(index):
        return slice(index * block, (index + 1) * block)

    keep = [[mask[c, a].astype(F32) for a in range(count)] for c in columns]
    trace = [jnp.zeros((1, 1), F32) for _ in columns]
    for w in range(window):
        x = margin(w)
        xt = x.T
        x_sq = total(x * x)
        for c in columns:
            a = w - c
            if 0 <= a < count:
                m = keep[c][a]
                y_h[c, :, at(a)], y_l[c, :, at(a)] = split(x * m)
                yt_h[c, at(a), :], yt_l[c, at(a), :] = split(xt * m)
                trace[c] = trace[c] + x_sq * m

    depth = piece * rep_size
    small_eye = eye(depth, depth)
    gram = [dot3((y_h[c], y_l[c]), (yt_h[c], yt_l[c])) for c in columns]
    coef = []
    kappa = []
    for c in columns:
        sum_sq = width + 2.0 * trace[c] + total(gram[c] * gram[c])
        s0 = 1.0 / (2.0 * jnp.sqrt(sum_sq / width))
        t0 = 1.5 - 0.5 * s0
        u0 = 1.5 - 0.5 * t0 * t0 * s0
        u1 = 0.5 * t0 * (t0 - s0)
        u2 = 0.5 * (0.25 * s0 - t0)
        u3 = 0.125
        root = jnp.sqrt(s0)
        factor = s0 * root
        e1 = (-t0 * u1 - 0.5 * u0) * factor
        e2 = (-t0 * u2 + 0.5 * u1) * factor
        e3 = (-t0 * u3 + 0.5 * u2) * factor
        e4 = 0.5 * u3 * factor
        unit[c] = jnp.broadcast_to(t0 * u0 * root, unit.shape[1:])
        coef.append((e1, e2, e3, e4))
        kappa.append(gram[c] * s0)
    kappa_s = [split(kappa[c]) for c in columns]
    square = [dot3(kappa_s[c], kappa_s[c]) for c in columns]
    cube = [dot3(kappa_s[c], split(square[c])) for c in columns]
    for c in columns:
        e1, e2, e3, e4 = coef[c]
        poly[c] = e1 * small_eye + e2 * kappa[c] + e3 * square[c] + e4 * cube[c]


def density_kernel(
    cols, reach, rep_size,
    even, mask, fermi, place,
    y_h, y_l, yt_h, yt_l, poly, unit, kept, far, near,
    out,
    ham, ham_h, ham_l, prod, shift_h, shift_l, sq_h, sq_l, side_h, side_l, whole,
):
    depth, width = y_h.shape[1:]
    count = 2 * reach + 1
    block = width // count
    window = cols + 2 * reach
    rows = width // rep_size
    columns = range(cols)
    cross = crossing(reach)
    is_even = even[0] == 1

    def at(index):
        return slice(index * block, (index + 1) * block)

    keep = [[mask[c, a].astype(F32) for a in range(count)] for c in columns]

    half = {}
    for side, base in ((0, 0), (1, reach + cols)):
        def read(index):
            if side == 0:
                return jnp.where(is_even, far[at(index)], near[at(index)])
            return jnp.where(is_even, near[at(index)], far[at(index)])

        end = slice((2 + len(cross)) * block, (2 + len(cross)) * block + 1)
        diagonal = jnp.where(is_even, far[end], near[end]) if side == 0 else jnp.where(is_even, near[end], far[end])
        mixed = read(0)
        one = jnp.where(upper(block), mixed, 0.0)
        two = mixed - one
        half[base, base] = one + two_sided(one, block)
        half[base + 1, base + 1] = two + two.T + diagonal * eye(block, block)
        half[base + 1, base] = read(1)
        for index, (i, j) in enumerate(cross):
            raw = read(2 + index)
            if side == 0:
                half[reach + j, i] = 0.5 * (raw + kept[3 + index].T)
            else:
                half[reach + cols + j, reach + i] = 0.5 * (kept[3 + len(cross) + index] + raw.T)
    half[reach, reach] = kept[0]
    half[reach + 1, reach] = kept[1]
    half[reach + 1, reach + 1] = kept[2]
    for a in range(window):
        for b in range(a + 1):
            if a - b <= reach:
                value = half[a, b]
                ham[at(a), at(b)] = value
                ham_h[at(a), at(b)], ham_l[at(a), at(b)] = split(value)
                if a != b:
                    value = value.T
                    ham[at(b), at(a)] = value
                    ham_h[at(b), at(a)], ham_l[at(b), at(a)] = split(value)
            else:
                none = jnp.zeros((block, block), BF16)
                for i, j in ((a, b), (b, a)):
                    ham_h[at(i), at(j)] = none
                    ham_l[at(i), at(j)] = none

    for c in columns:
        for begin, end in ((0, reach), (reach, reach + 1), (reach + 1, count)):
            low, high = max(0, begin - reach), min(count, end + reach)
            here = slice((c + begin) * block, (c + end) * block), slice((c + low) * block, (c + high) * block)
            inner = slice(low * block, high * block)
            side = dot3((ham_h[here], ham_l[here]), (yt_h[c, inner, :], yt_l[c, inner, :]))
            for a in range(begin, end):
                side_h[c, at(a), :], side_l[c, at(a), :] = split(side[at(a - begin)] * keep[c][a])
    core = [dot3((y_h[c], y_l[c]), (side_h[c], side_l[c])) for c in columns]

    poly_s = [split(poly[c]) for c in columns]
    core = [dot3(poly_s[c], split(core[c])) for c in columns]
    core = [dot3(split(core[c]), poly_s[c]) for c in columns]
    factor = []
    for c in columns:
        left = tuple(
            jnp.concatenate(pair, axis=1) for pair in ((side_h[c], yt_h[c]), (side_l[c], yt_l[c]))
        )
        right = split(jnp.concatenate([unit[c, 0:1, 0:1] * poly[c], 0.5 * core[c]], axis=0))
        factor.append(split(dot3(left, right)))
    for c in columns:
        prod[c] = dot3(factor[c], (y_h[c], y_l[c]))

    level = fermi[0] * eye(block, block)
    scale = []
    for c in columns:
        z0 = unit[c, 0:1, 0:1]
        z0_sq = z0 * z0
        sum_sq = jnp.zeros((block, block), F32)
        for a in range(count):
            for b in range(count):
                value = prod[c, at(a), at(b)] + prod[c, at(b), at(a)].T
                if abs(a - b) <= reach:
                    value = value + ham[at(c + a), at(c + b)] * (z0_sq * (keep[c][a] * keep[c][b]))
                if a == b:
                    value = value - level
                sum_sq = sum_sq + value * value
                if rows % PACKED:
                    whole[c, at(a), at(b)] = value
                high = value.astype(BF16)
                shift_h[c, at(a), at(b)] = high
                shift_l[c, at(a), at(b)] = (2.0 * (value - high.astype(F32))).astype(BF16)
        scale.append(1.0 / (4.0 * (total(sum_sq) / width + 1e-05)))

    for c in columns:
        high = shift_h[c]
        prod[c] = dot(
            jnp.concatenate([high, high], axis=1), jnp.concatenate([high, shift_l[c]], axis=0)
        )

    for c in columns:
        factor_c = 0.5 * scale[c]
        for a in range(count):
            for b in range(count):
                value = (prod[c, at(a), at(b)] + prod[c, at(b), at(a)].T) * factor_c
                sq_h[c, at(a), at(b)], sq_l[c, at(a), at(b)] = split(value)

    first = pl.multiple_of(place[0] * rows, rows)
    part_eye = eye(rows, width, first)
    own = pl.ds(first, rows)
    sq_s = [(sq_h[c], sq_l[c]) for c in columns]
    if rows % PACKED:
        x0 = [whole[c, own, :] for c in columns]
    else:
        x0 = [shift_h[c, own, :].astype(F32) + 0.5 * shift_l[c, own, :].astype(F32) for c in columns]
    x0 = [x0[c] * jnp.sqrt(scale[c]) for c in columns]
    x1 = [1.5 * x0[c] - 0.5 * dot3(split(x0[c]), sq_s[c]) for c in columns]
    y1 = [1.5 * x1[c] - 0.5 * dot3(split(x1[c]), sq_s[c]) for c in columns]
    y2 = [1.5 * y1[c] - 0.5 * dot3(split(y1[c]), sq_s[c]) for c in columns]
    for c in columns:
        y3 = dot3(split(y2[c]), sq_s[c])
        out[c] = 0.5 * (part_eye - (1.5 * x1[c] - 0.5 * y3))


def two_sided(one, block):
    return jnp.where(upper(block), 0.0, one.T)


def shaped(*shape, dtype=F32):
    return jax.ShapeDtypeStruct(shape, dtype)


SMEM = pl.BlockSpec(memory_space=pltpu.SMEM)
VMEM = pl.BlockSpec(memory_space=pltpu.VMEM)


def edges(even, band):
    cols, count, block, _ = band.shape
    reach = (count - 1) // 2
    cross = len(crossing(reach))
    height = (2 + cross) * block + TILE
    return pl.pallas_call(
        functools.partial(edge_kernel, reach),
        out_shape=[shaped(height, block), shaped(height, block), shaped(3 + 2 * cross, block, block)],
        in_specs=[SMEM, VMEM],
        out_specs=[VMEM] * 3,
        compiler_params=pltpu.CompilerParams(vmem_limit_bytes=8 * 2**20),
        cost_estimate=pl.CostEstimate(flops=0, bytes_accessed=4 * 2**20, transcendentals=0),
    )(even, band)


def inverse_root(even, mask, groups, nears, cols):
    rep_size = len(groups)
    piece, block = groups[0].shape[1:]
    reach = groups[0].shape[0] - cols
    depth = piece * rep_size
    width = (2 * reach + 1) * block
    return pl.pallas_call(
        functools.partial(root_kernel, cols, reach, rep_size),
        out_shape=[
            shaped(cols, depth, width, dtype=BF16),
            shaped(cols, depth, width, dtype=BF16),
            shaped(cols, width, depth, dtype=BF16),
            shaped(cols, width, depth, dtype=BF16),
            shaped(cols, depth, depth),
            shaped(cols, TILE, block),
        ],
        in_specs=[SMEM] * 2 + [VMEM] * (2 * rep_size),
        out_specs=[VMEM] * 6,
        compiler_params=pltpu.CompilerParams(vmem_limit_bytes=16 * 2**20),
        cost_estimate=pl.CostEstimate(flops=2**30, bytes_accessed=4 * 2**20, transcendentals=0),
    )(even, mask, *groups, *nears)


def density(even, mask, fermi, place, root, kept, far, near, reach, rep_size):
    cols, depth, width = root[0].shape
    rows = width // rep_size
    block = width // (2 * reach + 1)
    window = (cols + 2 * reach) * block
    return pl.pallas_call(
        functools.partial(density_kernel, cols, reach, rep_size),
        out_shape=shaped(cols, rows, width),
        in_specs=[SMEM] * 4 + [VMEM] * 9,
        out_specs=VMEM,
        scratch_shapes=[
            pltpu.VMEM((window, window), F32),
            pltpu.VMEM((window, window), BF16),
            pltpu.VMEM((window, window), BF16),
            pltpu.VMEM((cols, width, width), F32),
            pltpu.VMEM((cols, width, width), BF16),
            pltpu.VMEM((cols, width, width), BF16),
            pltpu.VMEM((cols, width, width), BF16),
            pltpu.VMEM((cols, width, width), BF16),
            pltpu.VMEM((cols, width, depth), BF16),
            pltpu.VMEM((cols, width, depth), BF16),
            pltpu.VMEM((cols, width, width) if rows % PACKED else (1, TILE, block), F32),
        ],
        compiler_params=pltpu.CompilerParams(vmem_limit_bytes=36 * 2**20),
        cost_estimate=pl.CostEstimate(flops=2**34, bytes_accessed=8 * 2**20, transcendentals=0),
    )(even, mask, fermi, place, *root, kept, far, near)


def near_swap(value):
    return lax.ppermute(value, "cols", [(i, i ^ 1) for i in range(lax.axis_size("cols"))])


def far_swap(value):
    count = lax.axis_size("cols")
    return lax.ppermute(value, "cols", [(i, (((i + 1) ^ 1) - 1) % count) for i in range(count)])


def rep_swap(value, step):
    return lax.ppermute(value, "rep", [(i, i ^ step) for i in range(lax.axis_size("rep"))])


def on_device(hamiltonian_band, margin_factors, neighbour_mask, fermi_level):
    cols, count, _, _ = hamiltonian_band.shape
    reach = (count - 1) // 2
    rep_size = lax.axis_size("rep")
    even = 1 - (lax.axis_index("cols").astype(jnp.int32) % 2).reshape(1)
    place = lax.axis_index("rep").astype(jnp.int32).reshape(1)
    margin_far = far_swap(margin_factors)
    margin_near = near_swap(margin_factors)
    to_far, to_near, kept = edges(even, hamiltonian_band)
    far, near = far_swap(to_far), near_swap(to_near)
    margin_far, _ = lax.optimization_barrier((margin_far, kept))
    group = jnp.concatenate([margin_factors, margin_far], axis=0)
    groups = [group] + [rep_swap(group, step) for step in range(1, rep_size)]
    nears = [margin_near] + [near_swap(value) for value in groups[1:]]
    root = inverse_root(even, neighbour_mask, groups, nears, cols)
    return density(even, neighbour_mask, fermi_level, place, root, kept, far, near, reach, rep_size)


def solution(mesh):
    in_specs = (P("cols", None, None, None), P("cols", "rep", None), P("cols", None), P())
    out_specs = P("cols", "rep", None)
    return jax.shard_map(
        on_device, mesh=mesh, in_specs=in_specs, out_specs=out_specs, check_vma=False
    )
```

time: 42.1 us -> 35.2 us (0.84)
  blocking collectives: 10.1 us -> 0 us
  starting transfers between devices: 5 us -> 11.6 us
  waiting for transfers between devices: 9.36 us -> 4.44 us
  Pallas kernels: 15.6 us -> 16.4 us
  local copies, waits for them, and re-layouts: 1.09 us -> 1.78 us
    all_gather x1 -> x0, blocking collectives: 10.1 us -> none  [on_device(): factors = lax.all_gather(margin_factors, 'rep', axis=1, tiled=True)]
    ppermute x4 -> x10, starting transfers between devices: 5 us -> 11.6 us  [the longest x2 6.71 us: far_swap(): lax.ppermute(value, 'cols', [(i, ((i + 1 ^ 1) - 1) % count) for i in rang...]
    ppermute x4 -> x10, waiting for transfers between devices: 9.36 us -> 4.44 us  [the longest x3 3.52 us: rep_swap(): lax.ppermute(value, 'rep', [(i, i ^ step) for i in range(lax.axis_size('r...]
    pallas_call x1 -> x3, Pallas kernels: 15.6 us -> 16.4 us  [the longest x1 13.8 us: density(): pl.pallas_call(functools.partial(density_kernel, cols, reach, rep_size),...]
    unnamed x4 -> x7, local copies, waits for them, and re-layouts: 1.09 us -> 1.77 us
  transfers between devices with their start and end apart: 4 -> 10, of which waited for: 2 -> 5; matrix products, arithmetic and copies ran while one was open for 0% -> 0% of each run, Pallas kernels for 0% -> 7%
where the time goes in v2:
time: 35.2 us; the launch traced here: 34.9 us
  Pallas kernels  16.4 us (47%)
  starting transfers between devices  11.6 us (33%)
  waiting for transfers between devices  4.44 us (13%)
  local copies, waits for them, and re-layouts  1.78 us (5%)
  between operations  0.7 us (2%)
    pallas_call x1, Pallas kernels, density(): pl.pallas_call(functools.partial(density_kernel, cols, reach, rep_size),...  13.8 us
    ppermute x2, starting transfers between devices, far_swap(): lax.ppermute(value, 'cols', [(i, ((i + 1 ^ 1) - 1) % count) for i in rang...  6.71 us
    ppermute x3, starting transfers between devices, rep_swap(): lax.ppermute(value, 'rep', [(i, i ^ step) for i in range(lax.axis_size('r...  3.86 us
    ppermute x3, waiting for transfers between devices, rep_swap(): lax.ppermute(value, 'rep', [(i, i ^ step) for i in range(lax.axis_size('r...  3.52 us
    pallas_call x1, Pallas kernels, inverse_root(): pl.pallas_call(functools.partial(root_kernel, cols, reach, rep_size), out...  2.44 us
    unnamed x7, local copies, waits for them, and re-layouts  1.77 us
    ppermute x5, starting transfers between devices, near_swap(): lax.ppermute(value, 'cols', [(i, i ^ 1) for i in range(lax.axis_size('col...  1.01 us
  transfers between devices with their start and end apart: 10, of which 5 were waited for; matrix products, arithmetic and copies ran while one was open for 0% of the time, Pallas kernels for 7%

profile of v2, /device:TPU:0, one launch (start us, length us, event | category | flops | bytes accessed | tf_op | source)
XLA Modules:
  0.0 34.9 jit_solution(9540223876176064308)
XLA Ops:
  0.0 4.5 %collective-permute-start = (f32[2,64,128]{2,1,0:T(8,128)}, f32[2,64,128]{2,1,0:T(8,128)S(1)}, u32[]{:S(2)}, u32[]{:S(2)}) collective-permute-start(f32[2,64,128]{2,1,0:T(8,128)} %param.5), channel_id=1, source_target_pairs={{0,28},{4,8},{8,4},{12,16},{16,12},{20,24},{24,20},{28,0},{1,29},{... | collective-permute-start | bytes 196616 | tf_op jit(solution)/shard_map/ppermute | solution.py:366
  4.5 0.0 collective-permute-start.4
  4.5 0.0 copy-start
  4.5 1.1 %copy-done = f32[2,5,128,128]{3,2,1,0:T(8,128)S(1)} copy-done((f32[2,5,128,128]{3,2,1,0:T(8,128)S(1)}, f32[2,5,128,128]{3,2,1,0:T(8,128)}, u32[]{:S(2)}) %copy-start) | copy-done | bytes 655384
  5.6 0.0 copy-start.2
  5.6 0.2 shard_map.46
  5.7 0.7 %copy-done.2 = f32[2,64,128]{2,1,0:T(8,128)S(1)} copy-done((f32[2,64,128]{2,1,0:T(8,128)S(1)}, f32[2,64,128]{2,1,0:T(8,128)}, u32[]{:S(2)}) %copy-start.2) | copy-done | bytes 65560
  6.4 0.3 collective-permute-done
  6.8 2.3 %collective-permute-start.1 = (f32[4,64,128]{2,1,0:T(8,128)S(1)}, f32[4,64,128]{2,1,0:T(8,128)S(1)}, u32[]{:S(2)}, u32[]{:S(2)}) collective-permute-start(f32[4,64,128]{2,1,0:T(8,128)S(1)} %constant_dynamic-update-slice_fusion.refs_0_), channel_id=1, source_target_pairs={{0,1},{1,0},{2,3},{3,2},{4,5},{5,4},{6,7},{7,6},{8,9},{9,8},{10,11... | collective-permute-start | bytes 393224 | tf_op jit(solution)/shard_map/ppermute | solution.py:370
  9.1 1.5 %collective-permute-start.2 = (f32[4,64,128]{2,1,0:T(8,128)S(1)}, f32[4,64,128]{2,1,0:T(8,128)S(1)}, u32[]{:S(2)}, u32[]{:S(2)}) collective-permute-start(f32[4,64,128]{2,1,0:T(8,128)S(1)} %constant_dynamic-update-slice_fusion.refs_0_), channel_id=1, source_target_pairs={{0,2},{1,3},{2,0},{3,1},{4,6},{5,7},{6,4},{7,5},{8,10},{9,11},{10,... | collective-permute-start | bytes 393224 | tf_op jit(solution)/shard_map/ppermute | solution.py:370
  10.6 0.0 collective-permute-start.3
  10.6 2.2 %collective-permute-start.8 = (f32[648,128]{1,0:T(8,128)S(1)}, f32[648,128]{1,0:T(8,128)S(1)}, u32[]{:S(2)}, u32[]{:S(2)}) collective-permute-start(f32[648,128]{1,0:T(8,128)S(1)} %get-tuple-element.23), channel_id=1, source_target_pairs={{0,28},{4,8},{8,4},{12,16},{16,12},{20,24},{24,20},{28,0},{1,29},{... | collective-permute-start | bytes 995336 | tf_op jit(solution)/shard_map/ppermute | solution.py:366
  12.8 0.0 collective-permute-done.4.refs_4_
  12.8 0.0 collective-permute-start.9
  12.9 0.0 collective-permute-done.1.refs_1_
  12.9 0.5 %collective-permute-start.5 = (f32[4,64,128]{2,1,0:T(8,128)S(1)}, f32[4,64,128]{2,1,0:T(8,128)S(1)}, u32[]{:S(2)}, u32[]{:S(2)}) collective-permute-start(f32[4,64,128]{2,1,0:T(8,128)S(1)} %collective-permute-done.1.refs_1_), channel_id=1, source_target_pairs={{0,4},{4,0},{8,12},{12,8},{16,20},{20,16},{24,28},{28,24},{1,5},{5... | collective-permute-start | bytes 393224 | tf_op jit(solution)/shard_map/ppermute | solution.py:361
  13.4 3.5 %collective-permute-done.2.refs_2_ = f32[4,64,128]{2,1,0:T(8,128)S(1)} collective-permute-done((f32[4,64,128]{2,1,0:T(8,128)S(1)}, f32[4,64,128]{2,1,0:T(8,128)S(1)}, u32[]{:S(2)}, u32[]{:S(2)}) %collective-permute-start.2) | collective-permute-done | bytes 131104 | tf_op jit(solution)/shard_map/ppermute | solution.py:370
  16.9 0.0 collective-permute-start.6
  16.9 0.0 collective-permute-done.3.refs_3_
  16.9 0.5 %collective-permute-start.7 = (f32[4,64,128]{2,1,0:T(8,128)S(1)}, f32[4,64,128]{2,1,0:T(8,128)S(1)}, u32[]{:S(2)}, u32[]{:S(2)}) collective-permute-start(f32[4,64,128]{2,1,0:T(8,128)S(1)} %collective-permute-done.3.refs_3_), channel_id=1, source_target_pairs={{0,4},{4,0},{8,12},{12,8},{16,20},{20,16},{24,28},{28,24},{1,5},{5... | collective-permute-start | bytes 393224 | tf_op jit(solution)/shard_map/ppermute | solution.py:361
  17.4 0.0 copy-start.1
  18.0 0.0 collective-permute-done.5.refs_5_
  18.1 0.2 collective-permute-done.6.refs_6_
  18.2 0.2 collective-permute-done.7.refs_7_
  18.4 0.0 copy-done.1
  18.4 2.4 %shard_map.47 = (bf16[2,256,640]{2,1,0:T(8,128)(2,1)S(1)}, bf16[2,256,640]{2,1,0:T(8,128)(2,1)S(1)}, bf16[2,640,256]{2,1,0:T(8,128)(2,1)S(1)}, bf16[2,640,256]{2...) custom-call(s32[1]{0:T(128)} %bitcast.even, s32[2,5]{1,0:T(2,128)S(1)} %copy-done.1, ...), custom_call_target="tpu_custom_call" | custom-call | flops 1073741824 | bytes 4194304 | tf_op jit(solution)/shard_map/pallas_call | solution.py:315
  20.9 0.2 collective-permute-done.8.far
  21.1 0.0 collective-permute-done.9.near
  21.1 13.8 %shard_map.48 = f32[2,160,640]{2,1,0:T(8,128)} custom-call(s32[1]{0:T(128)} %bitcast.even, s32[2,5]{1,0:T(2,128)S(1)} %copy-done.1, f32[1]{0:T(128)S(6)} %copy.6.fermi, s32[1]{0:T(128)} %bitcast.1.place, bf16[2,256,640]{2,1,0:T(8,128)(2,1)S(1)} %get-tuple-element.17.y_h, bf16[2,256,640]{2,1,0:T(8,128)(2,1)S(1)} %get-tuple-element.18.y_l, ...), custom_call_target="tpu_custom_call" | custom-call | flops 17179869184 | bytes 8388608 | tf_op jit(solution)/shard_map/pallas_call | solution.py:337
  (2 shorter events, 0.0 us)
Async XLA Ops:
  0.0 6.8 %collective-permute-start = (f32[2,64,128]{2,1,0:T(8,128)}, f32[2,64,128]{2,1,0:T(8,128)S(1)}, u32[]{:S(2)}, u32[]{:S(2)}) collective-permute-start(f32[2,64,128]{2,1,0:T(8,128)} %param.5), channel_id=1, source_target_pairs={{0,28},{4,8},{8,4},{12,16},{16,12},{20,24},{24,20},{28,0},{1,29},{... | collective-permute-start | bytes 196616 | tf_op jit(solution)/shard_map/ppermute | solution.py:366
  4.5 8.4 %collective-permute-start.4 = (f32[2,64,128]{2,1,0:T(8,128)}, f32[2,64,128]{2,1,0:T(8,128)S(1)}, u32[]{:S(2)}, u32[]{:S(2)}) collective-permute-start(f32[2,64,128]{2,1,0:T(8,128)} %param.5), channel_id=1, source_target_pairs={{0,4},{4,0},{8,12},{12,8},{16,20},{20,16},{24,28},{28,24},{1,5},{5... | collective-permute-start | bytes 196616 | tf_op jit(solution)/shard_map/ppermute | solution.py:361
  4.5 1.1 %copy-start = (f32[2,5,128,128]{3,2,1,0:T(8,128)S(1)}, f32[2,5,128,128]{3,2,1,0:T(8,128)}, u32[]{:S(2)}) copy-start(f32[2,5,128,128]{3,2,1,0:T(8,128)} %band.1) | copy-start | bytes 1966084
  5.6 0.8 %copy-start.2 = (f32[2,64,128]{2,1,0:T(8,128)S(1)}, f32[2,64,128]{2,1,0:T(8,128)}, u32[]{:S(2)}) copy-start(f32[2,64,128]{2,1,0:T(8,128)} %param.5) | copy-start | bytes 196612
  6.8 6.1 %collective-permute-start.1 = (f32[4,64,128]{2,1,0:T(8,128)S(1)}, f32[4,64,128]{2,1,0:T(8,128)S(1)}, u32[]{:S(2)}, u32[]{:S(2)}) collective-permute-start(f32[4,64,128]{2,1,0:T(8,128)S(1)} %constant_dynamic-update-slice_fusion.refs_0_), channel_id=1, source_target_pairs={{0,1},{1,0},{2,3},{3,2},{4,5},{5,4},{6,7},{7,6},{8,9},{9,8},{10,11... | collective-permute-start | bytes 393224 | tf_op jit(solution)/shard_map/ppermute | solution.py:370
  9.1 7.8 %collective-permute-start.2 = (f32[4,64,128]{2,1,0:T(8,128)S(1)}, f32[4,64,128]{2,1,0:T(8,128)S(1)}, u32[]{:S(2)}, u32[]{:S(2)}) collective-permute-start(f32[4,64,128]{2,1,0:T(8,128)S(1)} %constant_dynamic-update-slice_fusion.refs_0_), channel_id=1, source_target_pairs={{0,2},{1,3},{2,0},{3,1},{4,6},{5,7},{6,4},{7,5},{8,10},{9,11},{10,... | collective-permute-start | bytes 393224 | tf_op jit(solution)/shard_map/ppermute | solution.py:370
  10.6 6.3 %collective-permute-start.3 = (f32[4,64,128]{2,1,0:T(8,128)S(1)}, f32[4,64,128]{2,1,0:T(8,128)S(1)}, u32[]{:S(2)}, u32[]{:S(2)}) collective-permute-start(f32[4,64,128]{2,1,0:T(8,128)S(1)} %constant_dynamic-update-slice_fusion.refs_0_), channel_id=1, source_target_pairs={{0,3},{1,2},{2,1},{3,0},{4,7},{5,6},{6,5},{7,4},{8,11},{9,10},{10,... | collective-permute-start | bytes 393224 | tf_op jit(solution)/shard_map/ppermute | solution.py:370
  10.6 10.5 %collective-permute-start.8 = (f32[648,128]{1,0:T(8,128)S(1)}, f32[648,128]{1,0:T(8,128)S(1)}, u32[]{:S(2)}, u32[]{:S(2)}) collective-permute-start(f32[648,128]{1,0:T(8,128)S(1)} %get-tuple-element.23), channel_id=1, source_target_pairs={{0,28},{4,8},{8,4},{12,16},{16,12},{20,24},{24,20},{28,0},{1,29},{... | collective-permute-start | bytes 995336 | tf_op jit(solution)/shard_map/ppermute | solution.py:366
  12.8 8.3 %collective-permute-start.9 = (f32[648,128]{1,0:T(8,128)S(1)}, f32[648,128]{1,0:T(8,128)S(1)}, u32[]{:S(2)}, u32[]{:S(2)}) collective-permute-start(f32[648,128]{1,0:T(8,128)S(1)} %get-tuple-element.24), channel_id=1, source_target_pairs={{0,4},{4,0},{8,12},{12,8},{16,20},{20,16},{24,28},{28,24},{1,5},{5... | collective-permute-start | bytes 995336 | tf_op jit(solution)/shard_map/ppermute | solution.py:361
  12.9 5.2 %collective-permute-start.5 = (f32[4,64,128]{2,1,0:T(8,128)S(1)}, f32[4,64,128]{2,1,0:T(8,128)S(1)}, u32[]{:S(2)}, u32[]{:S(2)}) collective-permute-start(f32[4,64,128]{2,1,0:T(8,128)S(1)} %collective-permute-done.1.refs_1_), channel_id=1, source_target_pairs={{0,4},{4,0},{8,12},{12,8},{16,20},{20,16},{24,28},{28,24},{1,5},{5... | collective-permute-start | bytes 393224 | tf_op jit(solution)/shard_map/ppermute | solution.py:361
  16.9 1.3 %collective-permute-start.6 = (f32[4,64,128]{2,1,0:T(8,128)S(1)}, f32[4,64,128]{2,1,0:T(8,128)S(1)}, u32[]{:S(2)}, u32[]{:S(2)}) collective-permute-start(f32[4,64,128]{2,1,0:T(8,128)S(1)} %collective-permute-done.2.refs_2_), channel_id=1, source_target_pairs={{0,4},{4,0},{8,12},{12,8},{16,20},{20,16},{24,28},{28,24},{1,5},{5... | collective-permute-start | bytes 393224 | tf_op jit(solution)/shard_map/ppermute | solution.py:361
  16.9 1.5 %collective-permute-start.7 = (f32[4,64,128]{2,1,0:T(8,128)S(1)}, f32[4,64,128]{2,1,0:T(8,128)S(1)}, u32[]{:S(2)}, u32[]{:S(2)}) collective-permute-start(f32[4,64,128]{2,1,0:T(8,128)S(1)} %collective-permute-done.3.refs_3_), channel_id=1, source_target_pairs={{0,4},{4,0},{8,12},{12,8},{16,20},{20,16},{24,28},{28,24},{1,5},{5... | collective-permute-start | bytes 393224 | tf_op jit(solution)/shard_map/ppermute | solution.py:361
  17.4 1.0 %copy-start.1 = (s32[2,5]{1,0:T(2,128)S(1)}, s32[2,5]{1,0:T(2,128)}, u32[]{:S(2)}) copy-start(s32[2,5]{1,0:T(2,128)} %mask.3) | copy-start | bytes 124

commit v3 on v2

v3 whole, which is shorter than its diff:
```python
import functools

import jax
import jax.numpy as jnp
from jax import lax
from jax.experimental import pallas as pl
from jax.experimental.pallas import tpu as pltpu
from jax.sharding import PartitionSpec as P

F32 = jnp.float32
BF16 = jnp.bfloat16
PACKED = 16
STEP = 256
TILE = 8


def split(value):
    high = value.astype(BF16)
    return high, (value - high.astype(F32)).astype(BF16)


def dot(left, right):
    return jnp.dot(left, right, preferred_element_type=F32)


def dot3(left, right):
    (left_high, left_low), (right_high, right_low) = left, right
    return dot(
        jnp.concatenate([left_high, left_low, left_high], axis=1),
        jnp.concatenate([right_high, right_high, right_low], axis=0),
    )


def total(value):
    return jnp.sum(jnp.sum(value, axis=0, keepdims=True), axis=1, keepdims=True)


def eye(rows, columns, first=0):
    row = lax.broadcasted_iota(jnp.int32, (rows, columns), 0) + first
    column = lax.broadcasted_iota(jnp.int32, (rows, columns), 1)
    return jnp.where(row == column, 1.0, 0.0).astype(F32)


def upper(block):
    row = lax.broadcasted_iota(jnp.int32, (block, block), 0)
    return row <= lax.broadcasted_iota(jnp.int32, (block, block), 1)


def crossing(reach):
    return [(i, j) for j in range(reach) for i in range(reach) if reach + j - i <= reach]


def edge_kernel(reach, even, band, own, far, near, kept):
    block = band.shape[2]
    cross = crossing(reach)
    first = 0.5 * (band[0, reach] + band[0, reach].T)
    second = 0.5 * (band[1, reach] + band[1, reach].T)
    below = 0.5 * (band[0, reach + 1] + band[1, reach - 1].T)
    mixed = jnp.where(upper(block), first, second)
    diagonal = jnp.sum(second * eye(block, block), axis=0, keepdims=True)
    for out in (far, near):
        out[0:block] = mixed
        out[block : 2 * block] = below
        end = (2 + len(cross)) * block
        out[end : end + TILE] = jnp.broadcast_to(diagonal, (TILE, block))
    cols, piece, _ = own.shape
    for c in range(cols):
        begin = near.shape[0] + (c - cols) * piece
        near[begin : begin + piece] = own[c]
    kept[0] = first
    kept[1] = below
    kept[2] = second
    is_even = even[0] == 1
    for index, (i, j) in enumerate(cross):
        to_left = band[j, i - j]
        to_right = band[i, 2 * reach + j - i]
        here = slice((2 + index) * block, (3 + index) * block)
        far[here] = jnp.where(is_even, to_left, to_right)
        near[here] = jnp.where(is_even, to_right, to_left)
        kept[3 + index] = to_left
        kept[3 + len(cross) + index] = to_right


def root_kernel(cols, reach, rep_size, even, mask, *refs):
    owns = refs[:rep_size]
    fars = refs[rep_size : 2 * rep_size]
    nears = refs[2 * rep_size : 3 * rep_size]
    y_h, y_l, yt_h, yt_l, p_h, p_l, pt_h, pt_l, unit = refs[3 * rep_size :]
    piece, block = owns[0].shape[1:]
    count = 2 * reach + 1
    window = cols + 2 * reach
    width = count * block
    columns = range(cols)
    is_even = even[0] == 1

    def margin(w):
        parts = []
        for own, far, near in zip(owns, fars, nears):
            if reach <= w < reach + cols:
                parts.append(own[w - reach])
                continue
            index = w if w < reach else w - reach - cols
            from_far = far[far.shape[0] - cols + index]
            if len(near.shape) == 2:
                begin = near.shape[0] + (index - cols) * piece
                from_near = near[begin : begin + piece]
            else:
                from_near = near[index]
            pair = from_far, from_near
            parts.append(jnp.where(is_even, *(pair if w < reach else pair[::-1])))
        return jnp.concatenate(parts, axis=0)

    def at(index):
        return slice(index * block, (index + 1) * block)

    keep = [[mask[c, a].astype(F32) for a in range(count)] for c in columns]
    for w in range(window):
        x = margin(w)
        xt = x.T
        for c in columns:
            a = w - c
            if 0 <= a < count:
                m = keep[c][a]
                y_h[c, :, at(a)], y_l[c, :, at(a)] = split(x * m)
                yt_h[c, at(a), :], yt_l[c, at(a), :] = split(xt * m)

    depth = piece * rep_size
    small_eye = eye(depth, depth)
    gram = [dot3((y_h[c], y_l[c]), (yt_h[c], yt_l[c])) for c in columns]
    gram_s = [split(gram[c]) for c in columns]
    square = [dot3(gram_s[c], gram_s[c]) for c in columns]
    cube = [dot3(gram_s[c], split(square[c])) for c in columns]
    poly = []
    for c in columns:
        sum_sq = width + total(gram[c] * (gram[c] + 2.0 * small_eye))
        s0 = 1.0 / (2.0 * jnp.sqrt(sum_sq / width))
        t0 = 1.5 - 0.5 * s0
        u0 = 1.5 - 0.5 * t0 * t0 * s0
        u1 = 0.5 * t0 * (t0 - s0)
        u2 = 0.5 * (0.25 * s0 - t0)
        u3 = 0.125
        root = jnp.sqrt(s0)
        e1 = (-t0 * u1 - 0.5 * u0) * (root * s0)
        e2 = (-t0 * u2 + 0.5 * u1) * (root * s0 * s0)
        e3 = (-t0 * u3 + 0.5 * u2) * (root * s0 * s0 * s0)
        e4 = 0.5 * u3 * (root * s0 * s0 * s0 * s0)
        unit[c] = jnp.broadcast_to(t0 * u0 * root, unit.shape[1:])
        poly.append(split(e1 * small_eye + e2 * gram[c] + e3 * square[c] + e4 * cube[c]))
    for c in columns:
        p = dot3(poly[c], (y_h[c], y_l[c]))
        p_h[c], p_l[c] = split(p)
        for a in range(count):
            pt_h[c, at(a), :], pt_l[c, at(a), :] = split(p[:, at(a)].T)


def density_kernel(
    cols, reach, rep_size,
    even, mask, fermi, place,
    y_h, y_l, yt_h, yt_l, p_h, p_l, pt_h, pt_l, unit, kept, far, near,
    target,
    ham, ham_h, ham_l, whole, out, sent, *scratch,
):
    prod, shift_h, shift_l, sq_h, sq_l, cross_side, side_h, side_l, tail = (
        scratch[begin : begin + cols] for begin in range(0, 9 * cols, cols)
    )
    depth, width = y_h.shape[1:]
    count = 2 * reach + 1
    block = width // count
    window = cols + 2 * reach
    rows = width // rep_size
    columns = range(cols)
    cross = crossing(reach)
    is_even = even[0] == 1

    def at(index):
        return slice(index * block, (index + 1) * block)

    keep = [[mask[c, a].astype(F32) for a in range(count)] for c in columns]

    half = {}
    for side, base in ((0, 0), (1, reach + cols)):
        def read(index):
            if side == 0:
                return jnp.where(is_even, far[at(index)], near[at(index)])
            return jnp.where(is_even, near[at(index)], far[at(index)])

        end = slice((2 + len(cross)) * block, (2 + len(cross)) * block + 1)
        diagonal = jnp.where(is_even, far[end], near[end]) if side == 0 else jnp.where(is_even, near[end], far[end])
        mixed = read(0)
        one = jnp.where(upper(block), mixed, 0.0)
        two = mixed - one
        half[base, base] = one + two_sided(one, block)
        half[base + 1, base + 1] = two + two.T + diagonal * eye(block, block)
        half[base + 1, base] = read(1)
        for index, (i, j) in enumerate(cross):
            raw = read(2 + index)
            if side == 0:
                half[reach + j, i] = 0.5 * (raw + kept[3 + index].T)
            else:
                half[reach + cols + j, reach + i] = 0.5 * (kept[3 + len(cross) + index] + raw.T)
    half[reach, reach] = kept[0]
    half[reach + 1, reach] = kept[1]
    half[reach + 1, reach + 1] = kept[2]
    for a in range(window):
        for b in range(a + 1):
            if a - b <= reach:
                value = half[a, b]
                ham[at(a), at(b)] = value
                ham_h[at(a), at(b)], ham_l[at(a), at(b)] = split(value)
                if a != b:
                    value = value.T
                    ham[at(b), at(a)] = value
                    ham_h[at(b), at(a)], ham_l[at(b), at(a)] = split(value)
            else:
                none = jnp.zeros((block, block), BF16)
                for i, j in ((a, b), (b, a)):
                    ham_h[at(i), at(j)] = none
                    ham_l[at(i), at(j)] = none

    for c in columns:
        for begin, end in ((0, reach), (reach, reach + 1), (reach + 1, count)):
            low, high = max(0, begin - reach), min(count, end + reach)
            here = slice((c + begin) * block, (c + end) * block), slice((c + low) * block, (c + high) * block)
            inner = slice(low * block, high * block)
            part = dot3((ham_h[here], ham_l[here]), (pt_h[c, inner, :], pt_l[c, inner, :]))
            for a in range(begin, end):
                value = part[at(a - begin)] * keep[c][a]
                cross_side[c][at(a), :] = value
                side_h[c][at(a), :], side_l[c][at(a), :] = split(value)
    core = [split(dot3((p_h[c], p_l[c]), (side_h[c][...], side_l[c][...]))) for c in columns]

    factor = []
    for c in columns:
        value = unit[c, 0:1, 0:1] * cross_side[c][...] + 0.5 * dot3((yt_h[c], yt_l[c]), core[c])
        factor.append(split(value))
    for c in columns:
        prod[c][...] = dot3(factor[c], (y_h[c], y_l[c]))

    level = fermi[0] * eye(block, block)
    scale = []
    for c in columns:
        z0 = unit[c, 0:1, 0:1]
        z0_sq = z0 * z0
        sum_sq = jnp.zeros((block, block), F32)
        for a in range(count):
            for b in range(a + 1):
                value = prod[c][at(a), at(b)] + prod[c][at(b), at(a)].T
                if a - b <= reach:
                    value = value + ham[at(c + a), at(c + b)] * (z0_sq * (keep[c][a] * keep[c][b]))
                if a == b:
                    value = value - level
                sum_sq = sum_sq + value * value * (1.0 if a == b else 2.0)
                for i, j in ((a, b), (b, a))[: 1 + (a != b)]:
                    if (i, j) != (a, b):
                        value = value.T
                    if rows % PACKED:
                        whole[c, at(i), at(j)] = value
                    high = value.astype(BF16)
                    shift_h[c][at(i), at(j)] = high
                    shift_l[c][at(i), at(j)] = (2.0 * (value - high.astype(F32))).astype(BF16)
        scale.append(1.0 / (4.0 * (total(sum_sq) / width + 1e-05)))

    edge = width - block
    for c in columns:
        high, low = shift_h[c][...], shift_l[c][...]
        prod[c][:, :edge] = dot(
            jnp.concatenate([high, high], axis=1),
            jnp.concatenate([high[:, :edge], low[:, :edge]], axis=0),
        )
        tail[c][...] = dot(
            jnp.concatenate([high[edge:], low[edge:]], axis=1), jnp.concatenate([high, high], axis=0)
        )

    first = pl.multiple_of(place[0] * rows, rows)
    part_eye = eye(rows, width, first)
    own = pl.ds(first, rows)

    def scaled(c):
        factor_c = 0.5 * scale[c]
        for a in range(count):
            for b in range(a + 1):
                if a < count - 1:
                    value = prod[c][at(a), at(b)] + prod[c][at(b), at(a)].T
                elif b < a:
                    value = prod[c][at(a), at(b)] + tail[c][:, at(b)]
                else:
                    value = tail[c][:, at(b)]
                    value = value + value.T
                value = value * factor_c
                sq_h[c][at(a), at(b)], sq_l[c][at(a), at(b)] = split(value)
                if a != b:
                    sq_h[c][at(b), at(a)], sq_l[c][at(b), at(a)] = split(value.T)

    if rows % PACKED:
        x0 = [whole[c, own, :] for c in columns]
    else:
        x0 = [shift_h[c][own, :].astype(F32) + 0.5 * shift_l[c][own, :].astype(F32) for c in columns]
    x0 = [x0[c] * jnp.sqrt(scale[c]) for c in columns]
    sq_s, x1 = [], []
    for c in columns:
        scaled(c)
        sq_s.append((sq_h[c][...], sq_l[c][...]))
        x1.append(1.5 * x0[c] - 0.5 * dot3(split(x0[c]), sq_s[c]))
    y1 = [1.5 * x1[c] - 0.5 * dot3(split(x1[c]), sq_s[c]) for c in columns]
    y2 = [1.5 * y1[c] - 0.5 * dot3(split(y1[c]), sq_s[c]) for c in columns]
    copies = []
    for c in columns:
        left = split(y2[c])
        for index, begin in enumerate(range(0, width, STEP)):
            here = slice(begin, min(begin + STEP, width))
            y3 = dot3(left, (sq_h[c][:, here], sq_l[c][:, here]))
            out[c, :, here] = 0.5 * (part_eye[:, here] - (1.5 * x1[c][:, here] - 0.5 * y3))
            copies.append(
                pltpu.make_async_copy(out.at[c, :, here], target.at[c, :, here], sent.at[c, index])
            )
            copies[-1].start()
    for copy in copies:
        copy.wait()


def two_sided(one, block):
    return jnp.where(upper(block), 0.0, one.T)


def shaped(*shape, dtype=F32):
    return jax.ShapeDtypeStruct(shape, dtype)


SMEM = pl.BlockSpec(memory_space=pltpu.SMEM)
VMEM = pl.BlockSpec(memory_space=pltpu.VMEM)


def edges(even, band, own):
    cols, count, block, _ = band.shape
    reach = (count - 1) // 2
    cross = len(crossing(reach))
    height = (2 + cross) * block + TILE
    return pl.pallas_call(
        functools.partial(edge_kernel, reach),
        out_shape=[shaped(height, block), shaped(height + own.shape[0] * own.shape[1], block), shaped(3 + 2 * cross, block, block)],
        in_specs=[SMEM, VMEM, VMEM],
        out_specs=[VMEM] * 3,
        compiler_params=pltpu.CompilerParams(vmem_limit_bytes=8 * 2**20),
        cost_estimate=pl.CostEstimate(flops=0, bytes_accessed=4 * 2**20, transcendentals=0),
    )(even, band, own)


def inverse_root(even, mask, owns, fars, nears, reach):
    rep_size = len(owns)
    cols, piece, block = owns[0].shape
    depth = piece * rep_size
    width = (2 * reach + 1) * block
    return pl.pallas_call(
        functools.partial(root_kernel, cols, reach, rep_size),
        out_shape=[
            shaped(cols, depth, width, dtype=BF16),
            shaped(cols, depth, width, dtype=BF16),
            shaped(cols, width, depth, dtype=BF16),
            shaped(cols, width, depth, dtype=BF16),
            shaped(cols, depth, width, dtype=BF16),
            shaped(cols, depth, width, dtype=BF16),
            shaped(cols, width, depth, dtype=BF16),
            shaped(cols, width, depth, dtype=BF16),
            shaped(cols, TILE, block),
        ],
        in_specs=[SMEM] * 2 + [VMEM] * (3 * rep_size),
        out_specs=[VMEM] * 9,
        compiler_params=pltpu.CompilerParams(vmem_limit_bytes=16 * 2**20),
        cost_estimate=pl.CostEstimate(flops=2**30, bytes_accessed=4 * 2**20, transcendentals=0),
    )(even, mask, *owns, *fars, *nears)


def density(even, mask, fermi, place, root, kept, far, near, reach, rep_size):
    cols, depth, width = root[0].shape
    rows = width // rep_size
    block = width // (2 * reach + 1)
    window = (cols + 2 * reach) * block
    return pl.pallas_call(
        functools.partial(density_kernel, cols, reach, rep_size),
        out_shape=shaped(cols, rows, width),
        in_specs=[SMEM] * 4 + [VMEM] * 12,
        out_specs=pl.BlockSpec(memory_space=pl.ANY),
        scratch_shapes=[
            pltpu.VMEM((window, window), F32),
            pltpu.VMEM((window, window), BF16),
            pltpu.VMEM((window, window), BF16),
            pltpu.VMEM((cols, width, width) if rows % PACKED else (1, TILE, block), F32),
            pltpu.VMEM((cols, rows, width), F32),
            pltpu.SemaphoreType.DMA((cols, pl.cdiv(width, STEP))),
            *[pltpu.VMEM((width, width), F32)] * cols,
            *[pltpu.VMEM((width, width), BF16)] * (4 * cols),
            *[pltpu.VMEM((width, depth), F32)] * cols,
            *[pltpu.VMEM((width, depth), BF16)] * (2 * cols),
            *[pltpu.VMEM((block, width), F32)] * cols,
        ],
        compiler_params=pltpu.CompilerParams(vmem_limit_bytes=36 * 2**20),
        cost_estimate=pl.CostEstimate(flops=2**34, bytes_accessed=8 * 2**20, transcendentals=0),
    )(even, mask, fermi, place, *root, kept, far, near)


def near_swap(value):
    return lax.ppermute(value, "cols", [(i, i ^ 1) for i in range(lax.axis_size("cols"))])


def far_swap(value):
    count = lax.axis_size("cols")
    return lax.ppermute(value, "cols", [(i, (((i + 1) ^ 1) - 1) % count) for i in range(count)])


def rep_swap(value, step):
    return lax.ppermute(value, "rep", [(i, i ^ step) for i in range(lax.axis_size("rep"))])


def on_device(hamiltonian_band, margin_factors, neighbour_mask, fermi_level):
    cols, count, _, _ = hamiltonian_band.shape
    reach = (count - 1) // 2
    rep_size = lax.axis_size("rep")
    even = 1 - (lax.axis_index("cols").astype(jnp.int32) % 2).reshape(1)
    place = lax.axis_index("rep").astype(jnp.int32).reshape(1)
    margin_far = far_swap(margin_factors)
    to_far, to_near, kept = edges(even, hamiltonian_band, margin_factors)
    margin_far, _ = lax.optimization_barrier((margin_far, kept))
    far = far_swap(to_far)
    near = near_swap(to_near)
    group = jnp.concatenate([margin_factors, margin_far], axis=0)
    groups = [group] + [rep_swap(group, step) for step in range(1, rep_size)]
    owns = [margin_factors] + groups[1:]
    fars = [margin_far] + groups[1:]
    nears = [near] + [near_swap(value) for value in groups[1:]]
    root = inverse_root(even, neighbour_mask, owns, fars, nears, reach)
    return density(even, neighbour_mask, fermi_level, place, root, kept, far, near, reach, rep_size)


def solution(mesh):
    in_specs = (P("cols", None, None, None), P("cols", "rep", None), P("cols", None), P())
    out_specs = P("cols", "rep", None)
    return jax.shard_map(
        on_device, mesh=mesh, in_specs=in_specs, out_specs=out_specs, check_vma=False
    )
```

time: 35.2 us -> 33.9 us (0.963)
  Pallas kernels: 16.4 us -> 15.3 us
  starting transfers between devices: 11.6 us -> 10.6 us
  local copies, waits for them, and re-layouts: 1.78 us -> 2.53 us
    pallas_call x1, Pallas kernels: 13.8 us -> 12.1 us  [density(): pl.pallas_call(functools.partial(density_kernel, cols, reach, rep_size),...]
    unnamed x7 -> x9, local copies, waits for them, and re-layouts: 1.77 us -> 2.53 us
    pallas_call x1, Pallas kernels: 2.44 us -> 3.06 us  [inverse_root(): pl.pallas_call(functools.partial(root_kernel, cols, reach, rep_size), out...]
    ppermute x2, waiting for transfers between devices: 0.57 us -> 0.01 us  [far_swap(): lax.ppermute(value, 'cols', [(i, ((i + 1 ^ 1) - 1) % count) for i in rang...]
    ppermute x3, waiting for transfers between devices: 3.52 us -> 4.02 us  [rep_swap(): lax.ppermute(value, 'rep', [(i, i ^ step) for i in range(lax.axis_size('r...]
    ppermute x5 -> x4, starting transfers between devices: 1.01 us -> 0.58 us  [near_swap(): lax.ppermute(value, 'cols', [(i, i ^ 1) for i in range(lax.axis_size('col...]
  transfers between devices with their start and end apart: 10 -> 9, of which waited for: 5 -> 4; matrix products, arithmetic and copies ran while one was open for 0% -> 0% of each run, Pallas kernels for 7% -> 10%
where the time goes in v3:
time: 33.9 us; the launch traced here: 33.6 us
  Pallas kernels  15.3 us (45%)
  starting transfers between devices  10.6 us (31%)
  waiting for transfers between devices  4.37 us (13%)
  local copies, waits for them, and re-layouts  2.53 us (7%)
  between operations  0.73 us (2%)
    pallas_call x1, Pallas kernels, density(): pl.pallas_call(functools.partial(density_kernel, cols, reach, rep_size),...  12.1 us
    ppermute x2, starting transfers between devices, far_swap(): lax.ppermute(value, 'cols', [(i, ((i + 1 ^ 1) - 1) % count) for i in rang...  6.49 us
    ppermute x3, waiting for transfers between devices, rep_swap(): lax.ppermute(value, 'rep', [(i, i ^ step) for i in range(lax.axis_size('r...  4.02 us
    ppermute x3, starting transfers between devices, rep_swap(): lax.ppermute(value, 'rep', [(i, i ^ step) for i in range(lax.axis_size('r...  3.55 us
    pallas_call x1, Pallas kernels, inverse_root(): pl.pallas_call(functools.partial(root_kernel, cols, reach, rep_size), out...  3.06 us
    unnamed x9, local copies, waits for them, and re-layouts  2.53 us
  transfers between devices with their start and end apart: 9, of which 4 were waited for; matrix products, arithmetic and copies ran while one was open for 0% of the time, Pallas kernels for 10%

profile of v3, /device:TPU:0, one launch (start us, length us, event | category | flops | bytes accessed | tf_op | source)
XLA Modules:
  0.0 33.6 jit_solution(1658493231653079989)
XLA Ops:
  0.0 4.5 %collective-permute-start = (f32[2,64,128]{2,1,0:T(8,128)}, f32[2,64,128]{2,1,0:T(8,128)S(1)}, u32[]{:S(2)}, u32[]{:S(2)}) collective-permute-start(f32[2,64,128]{2,1,0:T(8,128)} %refs_0_.1), channel_id=1, source_target_pairs={{0,28},{4,8},{8,4},{12,16},{16,12},{20,24},{24,20},{28,0},{1,29},{... | collective-permute-start | bytes 196616 | tf_op jit(solution)/shard_map/ppermute | solution.py:407
  4.5 0.0 copy-start
  4.5 1.1 %copy-done = f32[2,5,128,128]{3,2,1,0:T(8,128)S(1)} copy-done((f32[2,5,128,128]{3,2,1,0:T(8,128)S(1)}, f32[2,5,128,128]{3,2,1,0:T(8,128)}, u32[]{:S(2)}) %copy-start) | copy-done | bytes 655384
  5.6 0.0 copy-start.1
  5.6 0.8 %copy-done.1 = f32[2,64,128]{2,1,0:T(8,128)S(1)} copy-done((f32[2,64,128]{2,1,0:T(8,128)S(1)}, f32[2,64,128]{2,1,0:T(8,128)}, u32[]{:S(2)}) %copy-start.1) | copy-done | bytes 65560
  6.4 0.0 copy-start.2
  6.4 0.2 shard_map.46
  6.6 0.1 collective-permute-start.4
  6.7 0.6 %copy-done.2 = f32[2,64,128]{2,1,0:T(8,128)S(1)} copy-done((f32[2,64,128]{2,1,0:T(8,128)S(1)}, f32[2,64,128]{2,1,0:T(8,128)}, u32[]{:S(2)}) %copy-start.2) | copy-done | bytes 65560
  7.3 0.0 collective-permute-done.refs_4_
  7.3 1.8 %collective-permute-start.1 = (f32[4,64,128]{2,1,0:T(8,128)S(1)}, f32[4,64,128]{2,1,0:T(8,128)S(1)}, u32[]{:S(2)}, u32[]{:S(2)}) collective-permute-start(f32[4,64,128]{2,1,0:T(8,128)S(1)} %constant_dynamic-update-slice_fusion), channel_id=1, source_target_pairs={{0,1},{1,0},{2,3},{3,2},{4,5},{5,4},{6,7},{7,6},{8,9},{9,8},{10,11... | collective-permute-start | bytes 393224 | tf_op jit(solution)/shard_map/ppermute | solution.py:411
  9.1 1.5 %collective-permute-start.2 = (f32[4,64,128]{2,1,0:T(8,128)S(1)}, f32[4,64,128]{2,1,0:T(8,128)S(1)}, u32[]{:S(2)}, u32[]{:S(2)}) collective-permute-start(f32[4,64,128]{2,1,0:T(8,128)S(1)} %constant_dynamic-update-slice_fusion), channel_id=1, source_target_pairs={{0,2},{1,3},{2,0},{3,1},{4,6},{5,7},{6,4},{7,5},{8,10},{9,11},{10,... | collective-permute-start | bytes 393224 | tf_op jit(solution)/shard_map/ppermute | solution.py:411
  10.6 0.2 collective-permute-start.3
  10.8 2.0 %collective-permute-start.8 = (f32[648,128]{1,0:T(8,128)S(1)}, f32[648,128]{1,0:T(8,128)S(1)}, u32[]{:S(2)}, u32[]{:S(2)}) collective-permute-start(f32[648,128]{1,0:T(8,128)S(1)} %get-tuple-element.30), channel_id=1, source_target_pairs={{0,28},{4,8},{8,4},{12,16},{16,12},{20,24},{24,20},{28,0},{1,29},{... | collective-permute-start | bytes 995336 | tf_op jit(solution)/shard_map/ppermute | solution.py:407
  12.8 0.2 collective-permute-done.1.refs_1_.refs_5_
  13.0 0.0 collective-permute-start.5
  13.0 3.8 %collective-permute-done.2.refs_2_.refs_6_ = f32[4,64,128]{2,1,0:T(8,128)S(1)} collective-permute-done((f32[4,64,128]{2,1,0:T(8,128)S(1)}, f32[4,64,128]{2,1,0:T(8,128)S(1)}, u32[]{:S(2)}, u32[]{:S(2)}) %collective-permute-start.2) | collective-permute-done | bytes 131104 | tf_op jit(solution)/shard_map/ppermute | solution.py:411
  16.9 0.0 collective-permute-start.6
  16.9 0.0 collective-permute-done.3.refs_3_.refs_7_
  16.9 0.5 %collective-permute-start.7 = (f32[4,64,128]{2,1,0:T(8,128)S(1)}, f32[4,64,128]{2,1,0:T(8,128)S(1)}, u32[]{:S(2)}, u32[]{:S(2)}) collective-permute-start(f32[4,64,128]{2,1,0:T(8,128)S(1)} %collective-permute-done.3.refs_3_.refs_7_), channel_id=1, source_target_pairs={{0,4},{4,0},{8,12},{12,8},{16,20},{20,16},{24,28},{28,24},{1,5},{5... | collective-permute-start | bytes 393224 | tf_op jit(solution)/shard_map/ppermute | solution.py:402
  17.4 0.0 copy-start.3
  18.0 0.0 collective-permute-done.5.refs_9_
  18.1 0.2 collective-permute-done.6.refs_10_
  18.2 0.2 collective-permute-done.7.refs_11_
  18.4 0.0 collective-permute-done.4.refs_8_.near
  18.4 0.0 copy-done.3
  18.4 3.1 %shard_map.47 = (bf16[2,256,640]{2,1,0:T(8,128)(2,1)S(1)}, bf16[2,256,640]{2,1,0:T(8,128)(2,1)S(1)}, bf16[2,640,256]{2,1,0:T(8,128)(2,1)S(1)}, bf16[2,640,256]{2...) custom-call(s32[1]{0:T(128)} %bitcast.even, ...), custom_call_target="tpu_custom_call" | custom-call | flops 1073741824 | bytes 4194304 | tf_op jit(solution)/shard_map/pallas_call | solution.py:353
  21.5 0.0 collective-permute-done.8.far
  21.5 12.1 %shard_map.48 = f32[2,160,640]{2,1,0:T(8,128)} custom-call(s32[1]{0:T(128)} %bitcast.even, s32[2,5]{1,0:T(2,128)S(1)} %copy-done.3, f32[1]{0:T(128)S(6)} %copy.6.fermi, s32[1]{0:T(128)} %bitcast.1.place, bf16[2,256,640]{2,1,0:T(8,128)(2,1)S(1)} %get-tuple-element.21.y_h, bf16[2,256,640]{2,1,0:T(8,128)(2,1)S(1)} %get-tuple-element.22.y_l, ...), custom_call_target="tpu_custom_call" | custom-call | flops 17179869184 | bytes 8388608 | tf_op jit(solution)/shard_map/pallas_call | solution.py:378
  (2 shorter events, 0.0 us)
Async XLA Ops:
  0.0 7.3 %collective-permute-start = (f32[2,64,128]{2,1,0:T(8,128)}, f32[2,64,128]{2,1,0:T(8,128)S(1)}, u32[]{:S(2)}, u32[]{:S(2)}) collective-permute-start(f32[2,64,128]{2,1,0:T(8,128)} %refs_0_.1), channel_id=1, source_target_pairs={{0,28},{4,8},{8,4},{12,16},{16,12},{20,24},{24,20},{28,0},{1,29},{... | collective-permute-start | bytes 196616 | tf_op jit(solution)/shard_map/ppermute | solution.py:407
  4.5 1.1 %copy-start = (f32[2,5,128,128]{3,2,1,0:T(8,128)S(1)}, f32[2,5,128,128]{3,2,1,0:T(8,128)}, u32[]{:S(2)}) copy-start(f32[2,5,128,128]{3,2,1,0:T(8,128)} %band.1) | copy-start | bytes 1966084
  5.6 0.8 %copy-start.1 = (f32[2,64,128]{2,1,0:T(8,128)S(1)}, f32[2,64,128]{2,1,0:T(8,128)}, u32[]{:S(2)}) copy-start(f32[2,64,128]{2,1,0:T(8,128)} %refs_0_.1) | copy-start | bytes 196612
  6.4 0.8 %copy-start.2 = (f32[2,64,128]{2,1,0:T(8,128)S(1)}, f32[2,64,128]{2,1,0:T(8,128)}, u32[]{:S(2)}) copy-start(f32[2,64,128]{2,1,0:T(8,128)} %refs_0_.1) | copy-start | bytes 196612
  6.6 11.8 %collective-permute-start.4 = (f32[776,128]{1,0:T(8,128)S(1)}, f32[776,128]{1,0:T(8,128)S(1)}, u32[]{:S(2)}, u32[]{:S(2)}) collective-permute-start(f32[776,128]{1,0:T(8,128)S(1)} %get-tuple-element.20), channel_id=1, source_target_pairs={{0,4},{4,0},{8,12},{12,8},{16,20},{20,16},{24,28},{28,24},{1,5},{5... | collective-permute-start | bytes 1191944 | tf_op jit(solution)/shard_map/ppermute | solution.py:402
  7.3 5.8 %collective-permute-start.1 = (f32[4,64,128]{2,1,0:T(8,128)S(1)}, f32[4,64,128]{2,1,0:T(8,128)S(1)}, u32[]{:S(2)}, u32[]{:S(2)}) collective-permute-start(f32[4,64,128]{2,1,0:T(8,128)S(1)} %constant_dynamic-update-slice_fusion), channel_id=1, source_target_pairs={{0,1},{1,0},{2,3},{3,2},{4,5},{5,4},{6,7},{7,6},{8,9},{9,8},{10,11... | collective-permute-start | bytes 393224 | tf_op jit(solution)/shard_map/ppermute | solution.py:411
  9.1 7.8 %collective-permute-start.2 = (f32[4,64,128]{2,1,0:T(8,128)S(1)}, f32[4,64,128]{2,1,0:T(8,128)S(1)}, u32[]{:S(2)}, u32[]{:S(2)}) collective-permute-start(f32[4,64,128]{2,1,0:T(8,128)S(1)} %constant_dynamic-update-slice_fusion), channel_id=1, source_target_pairs={{0,2},{1,3},{2,0},{3,1},{4,6},{5,7},{6,4},{7,5},{8,10},{9,11},{10,... | collective-permute-start | bytes 393224 | tf_op jit(solution)/shard_map/ppermute | solution.py:411
  10.6 6.3 %collective-permute-start.3 = (f32[4,64,128]{2,1,0:T(8,128)S(1)}, f32[4,64,128]{2,1,0:T(8,128)S(1)}, u32[]{:S(2)}, u32[]{:S(2)}) collective-permute-start(f32[4,64,128]{2,1,0:T(8,128)S(1)} %constant_dynamic-update-slice_fusion), channel_id=1, source_target_pairs={{0,3},{1,2},{2,1},{3,0},{4,7},{5,6},{6,5},{7,4},{8,11},{9,10},{10,... | collective-permute-start | bytes 393224 | tf_op jit(solution)/shard_map/ppermute | solution.py:411
  10.8 10.6 %collective-permute-start.8 = (f32[648,128]{1,0:T(8,128)S(1)}, f32[648,128]{1,0:T(8,128)S(1)}, u32[]{:S(2)}, u32[]{:S(2)}) collective-permute-start(f32[648,128]{1,0:T(8,128)S(1)} %get-tuple-element.30), channel_id=1, source_target_pairs={{0,28},{4,8},{8,4},{12,16},{16,12},{20,24},{24,20},{28,0},{1,29},{... | collective-permute-start | bytes 995336 | tf_op jit(solution)/shard_map/ppermute | solution.py:407
  13.0 5.0 %collective-permute-start.5 = (f32[4,64,128]{2,1,0:T(8,128)S(1)}, f32[4,64,128]{2,1,0:T(8,128)S(1)}, u32[]{:S(2)}, u32[]{:S(2)}) collective-permute-start(f32[4,64,128]{2,1,0:T(8,128)S(1)} %collective-permute-done.1.refs_1_.refs_5_), channel_id=1, source_target_pairs={{0,4},{4,0},{8,12},{12,8},{16,20},{20,16},{24,28},{28,24},{1,5},{5... | collective-permute-start | bytes 393224 | tf_op jit(solution)/shard_map/ppermute | solution.py:402
  16.9 1.3 %collective-permute-start.6 = (f32[4,64,128]{2,1,0:T(8,128)S(1)}, f32[4,64,128]{2,1,0:T(8,128)S(1)}, u32[]{:S(2)}, u32[]{:S(2)}) collective-permute-start(f32[4,64,128]{2,1,0:T(8,128)S(1)} %collective-permute-done.2.refs_2_.refs_6_), channel_id=1, source_target_pairs={{0,4},{4,0},{8,12},{12,8},{16,20},{20,16},{24,28},{28,24},{1,5},{5... | collective-permute-start | bytes 393224 | tf_op jit(solution)/shard_map/ppermute | solution.py:402
  16.9 1.5 %collective-permute-start.7 = (f32[4,64,128]{2,1,0:T(8,128)S(1)}, f32[4,64,128]{2,1,0:T(8,128)S(1)}, u32[]{:S(2)}, u32[]{:S(2)}) collective-permute-start(f32[4,64,128]{2,1,0:T(8,128)S(1)} %collective-permute-done.3.refs_3_.refs_7_), channel_id=1, source_target_pairs={{0,4},{4,0},{8,12},{12,8},{16,20},{20,16},{24,28},{28,24},{1,5},{5... | collective-permute-start | bytes 393224 | tf_op jit(solution)/shard_map/ppermute | solution.py:402
  17.4 1.0 %copy-start.3 = (s32[2,5]{1,0:T(2,128)S(1)}, s32[2,5]{1,0:T(2,128)}, u32[]{:S(2)}) copy-start(s32[2,5]{1,0:T(2,128)} %mask.3) | copy-start | bytes 124

commit v4 on v3

--- a/solution.py
+++ b/solution.py
@@ -50,7 +50,7 @@
     return [(i, j) for j in range(reach) for i in range(reach) if reach + j - i <= reach]
 
 
-def edge_kernel(reach, even, band, own, far, near, kept):
+def edge_kernel(reach, even, band, own, far, near, kept, group):
     block = band.shape[2]
     cross = crossing(reach)
     first = 0.5 * (band[0, reach] + band[0, reach].T)
@@ -65,6 +65,7 @@
         out[end : end + TILE] = jnp.broadcast_to(diagonal, (TILE, block))
     cols, piece, _ = own.shape
     for c in range(cols):
+        group[c] = own[c]
         begin = near.shape[0] + (c - cols) * piece
         near[begin : begin + piece] = own[c]
     kept[0] = first
@@ -224,17 +225,18 @@
             inner = slice(low * block, high * block)
             part = dot3((ham_h[here], ham_l[here]), (pt_h[c, inner, :], pt_l[c, inner, :]))
             for a in range(begin, end):
-                value = part[at(a - begin)] * keep[c][a]
+                value = part[at(a - begin)]
                 cross_side[c][at(a), :] = value
                 side_h[c][at(a), :], side_l[c][at(a), :] = split(value)
     core = [split(dot3((p_h[c], p_l[c]), (side_h[c][...], side_l[c][...]))) for c in columns]
-
-    factor = []
-    for c in columns:
-        value = unit[c, 0:1, 0:1] * cross_side[c][...] + 0.5 * dot3((yt_h[c], yt_l[c]), core[c])
-        factor.append(split(value))
-    for c in columns:
-        prod[c][...] = dot3(factor[c], (y_h[c], y_l[c]))
+    for c in columns:
+        for a in range(count):
+            value = (unit[c, 0:1, 0:1] * keep[c][a]) * cross_side[c][at(a), :] + 0.5 * dot3(
+                (yt_h[c, at(a), :], yt_l[c, at(a), :]), core[c]
+            )
+            side_h[c][at(a), :], side_l[c][at(a), :] = split(value)
+    for c in columns:
+        prod[c][...] = dot3((side_h[c][...], side_l[c][...]), (y_h[c], y_l[c]))
 
     level = fermi[0] * eye(block, block)
     scale = []
@@ -261,7 +263,13 @@
         scale.append(1.0 / (4.0 * (total(sum_sq) / width + 1e-05)))
 
     edge = width - block
-    for c in columns:
+    first = pl.multiple_of(place[0] * rows, rows)
+    part_eye = eye(rows, width, first)
+    own = pl.ds(first, rows)
+    rows_of = [{} for _ in columns]
+    copies = []
+
+    def squared(c):
         high, low = shift_h[c][...], shift_l[c][...]
         prod[c][:, :edge] = dot(
             jnp.concatenate([high, high], axis=1),
@@ -270,10 +278,6 @@
         tail[c][...] = dot(
             jnp.concatenate([high[edge:], low[edge:]], axis=1), jnp.concatenate([high, high], axis=0)
         )
-
-    first = pl.multiple_of(place[0] * rows, rows)
-    part_eye = eye(rows, width, first)
-    own = pl.ds(first, rows)
 
     def scaled(c):
         factor_c = 0.5 * scale[c]
@@ -291,29 +295,41 @@
                 if a != b:
                     sq_h[c][at(b), at(a)], sq_l[c][at(b), at(a)] = split(value.T)
 
-    if rows % PACKED:
-        x0 = [whole[c, own, :] for c in columns]
-    else:
-        x0 = [shift_h[c][own, :].astype(F32) + 0.5 * shift_l[c][own, :].astype(F32) for c in columns]
-    x0 = [x0[c] * jnp.sqrt(scale[c]) for c in columns]
-    sq_s, x1 = [], []
-    for c in columns:
-        scaled(c)
-        sq_s.append((sq_h[c][...], sq_l[c][...]))
-        x1.append(1.5 * x0[c] - 0.5 * dot3(split(x0[c]), sq_s[c]))
-    y1 = [1.5 * x1[c] - 0.5 * dot3(split(x1[c]), sq_s[c]) for c in columns]
-    y2 = [1.5 * y1[c] - 0.5 * dot3(split(y1[c]), sq_s[c]) for c in columns]
-    copies = []
-    for c in columns:
-        left = split(y2[c])
+    def step(c, source, target_name):
+        value = rows_of[c][source]
+        rows_of[c][target_name] = 1.5 * value - 0.5 * dot3(split(value), (sq_h[c][...], sq_l[c][...]))
+
+    def start(c):
+        if rows % PACKED:
+            value = whole[c, own, :]
+        else:
+            value = shift_h[c][own, :].astype(F32) + 0.5 * shift_l[c][own, :].astype(F32)
+        rows_of[c]["x0"] = value * jnp.sqrt(scale[c])
+        step(c, "x0", "x1")
+
+    def finish(c):
+        left = split(rows_of[c]["y2"])
         for index, begin in enumerate(range(0, width, STEP)):
             here = slice(begin, min(begin + STEP, width))
             y3 = dot3(left, (sq_h[c][:, here], sq_l[c][:, here]))
-            out[c, :, here] = 0.5 * (part_eye[:, here] - (1.5 * x1[c][:, here] - 0.5 * y3))
+            out[c, :, here] = 0.5 * (part_eye[:, here] - (1.5 * rows_of[c]["x1"][:, here] - 0.5 * y3))
             copies.append(
                 pltpu.make_async_copy(out.at[c, :, here], target.at[c, :, here], sent.at[c, index])
             )
             copies[-1].start()
+
+    stages = [
+        squared,
+        scaled,
+        start,
+        lambda c: step(c, "x1", "y1"),
+        lambda c: step(c, "y1", "y2"),
+        finish,
+    ]
+    for index in range(len(stages) + cols - 1):
+        for c in columns:
+            if 0 <= index - c < len(stages):
+                stages[index - c](c)
     for copy in copies:
         copy.wait()
 
@@ -337,9 +353,9 @@
     height = (2 + cross) * block + TILE
     return pl.pallas_call(
         functools.partial(edge_kernel, reach),
-        out_shape=[shaped(height, block), shaped(height + own.shape[0] * own.shape[1], block), shaped(3 + 2 * cross, block, block)],
+        out_shape=[shaped(height, block), shaped(height + own.shape[0] * own.shape[1], block), shaped(3 + 2 * cross, block, block), shaped(cols, *own.shape[1:])],
         in_specs=[SMEM, VMEM, VMEM],
-        out_specs=[VMEM] * 3,
+        out_specs=[VMEM] * 4,
         compiler_params=pltpu.CompilerParams(vmem_limit_bytes=8 * 2**20),
         cost_estimate=pl.CostEstimate(flops=0, bytes_accessed=4 * 2**20, transcendentals=0),
     )(even, band, own)
@@ -418,13 +434,12 @@
     even = 1 - (lax.axis_index("cols").astype(jnp.int32) % 2).reshape(1)
     place = lax.axis_index("rep").astype(jnp.int32).reshape(1)
     margin_far = far_swap(margin_factors)
-    to_far, to_near, kept = edges(even, hamiltonian_band, margin_factors)
-    margin_far, _ = lax.optimization_barrier((margin_far, kept))
+    to_far, to_near, kept, own = edges(even, hamiltonian_band, margin_factors)
     far = far_swap(to_far)
     near = near_swap(to_near)
-    group = jnp.concatenate([margin_factors, margin_far], axis=0)
+    group = jnp.concatenate([own, margin_far], axis=0)
     groups = [group] + [rep_swap(group, step) for step in range(1, rep_size)]
-    owns = [margin_factors] + groups[1:]
+    owns = [own] + groups[1:]
     fars = [margin_far] + groups[1:]
     nears = [near] + [near_swap(value) for value in groups[1:]]
     root = inverse_root(even, neighbour_mask, owns, fars, nears, reach)

time: 33.9 us -> 33.8 us (level)
  starting transfers between devices: 10.6 us -> 11.2 us
  local copies, waits for them, and re-layouts: 2.53 us -> 1.94 us
    unnamed x9 -> x7, local copies, waits for them, and re-layouts: 2.53 us -> 1.94 us
  transfers between devices with their start and end apart: 9 -> 9, of which waited for: 4 -> 5; matrix products, arithmetic and copies ran while one was open for 0% -> 0% of each run, Pallas kernels for 10% -> 10%
where the time goes in v4:
time: 33.8 us; the launch traced here: 33.6 us
  Pallas kernels  15.3 us (45%)
  starting transfers between devices  11.2 us (33%)
  waiting for transfers between devices  4.44 us (13%)
  local copies, waits for them, and re-layouts  1.94 us (6%)
  between operations  0.72 us (2%)
    pallas_call x1, Pallas kernels, density(): pl.pallas_call(functools.partial(density_kernel, cols, reach, rep_size),...  12.1 us
    ppermute x2, starting transfers between devices, far_swap(): lax.ppermute(value, 'cols', [(i, ((i + 1 ^ 1) - 1) % count) for i in rang...  6.71 us
    ppermute x3, waiting for transfers between devices, rep_swap(): lax.ppermute(value, 'rep', [(i, i ^ step) for i in range(lax.axis_size('r...  4.02 us
    ppermute x3, starting transfers between devices, rep_swap(): lax.ppermute(value, 'rep', [(i, i ^ step) for i in range(lax.axis_size('r...  3.86 us
    pallas_call x1, Pallas kernels, inverse_root(): pl.pallas_call(functools.partial(root_kernel, cols, reach, rep_size), out...  3.06 us
    unnamed x7, local copies, waits for them, and re-layouts  1.94 us
  transfers between devices with their start and end apart: 9, of which 5 were waited for; matrix products, arithmetic and copies ran while one was open for 0% of the time, Pallas kernels for 10%

profile of v4, /device:TPU:0, one launch (start us, length us, event | category | flops | bytes accessed | tf_op | source)
XLA Modules:
  0.0 33.6 jit_solution(14589343585975775926)
XLA Ops:
  0.0 4.5 %collective-permute-start = (f32[2,64,128]{2,1,0:T(8,128)}, f32[2,64,128]{2,1,0:T(8,128)S(1)}, u32[]{:S(2)}, u32[]{:S(2)}) collective-permute-start(f32[2,64,128]{2,1,0:T(8,128)} %own.1), channel_id=1, source_target_pairs={{0,28},{4,8},{8,4},{12,16},{16,12},{20,24},{24,20},{28,0},{1,29},{... | collective-permute-start | bytes 196616 | tf_op jit(solution)/shard_map/ppermute | solution.py:423
  4.5 0.0 copy-start
  4.5 1.1 %copy-done = f32[2,5,128,128]{3,2,1,0:T(8,128)S(1)} copy-done((f32[2,5,128,128]{3,2,1,0:T(8,128)S(1)}, f32[2,5,128,128]{3,2,1,0:T(8,128)}, u32[]{:S(2)}) %copy-start) | copy-done | bytes 655384
  5.6 0.0 copy-start.1
  5.6 0.8 %copy-done.1 = f32[2,64,128]{2,1,0:T(8,128)S(1)} copy-done((f32[2,64,128]{2,1,0:T(8,128)S(1)}, f32[2,64,128]{2,1,0:T(8,128)}, u32[]{:S(2)}) %copy-start.1) | copy-done | bytes 65560
  6.4 0.2 shard_map.46
  6.6 0.1 collective-permute-start.4
  6.7 0.1 collective-permute-done.refs_4_
  6.8 2.3 %collective-permute-start.1 = (f32[4,64,128]{2,1,0:T(8,128)S(1)}, f32[4,64,128]{2,1,0:T(8,128)S(1)}, u32[]{:S(2)}, u32[]{:S(2)}) collective-permute-start(f32[4,64,128]{2,1,0:T(8,128)S(1)} %constant_dynamic-update-slice_fusion), channel_id=1, source_target_pairs={{0,1},{1,0},{2,3},{3,2},{4,5},{5,4},{6,7},{7,6},{8,9},{9,8},{10,11... | collective-permute-start | bytes 393224 | tf_op jit(solution)/shard_map/ppermute | solution.py:427
  9.1 1.5 %collective-permute-start.2 = (f32[4,64,128]{2,1,0:T(8,128)S(1)}, f32[4,64,128]{2,1,0:T(8,128)S(1)}, u32[]{:S(2)}, u32[]{:S(2)}) collective-permute-start(f32[4,64,128]{2,1,0:T(8,128)S(1)} %constant_dynamic-update-slice_fusion), channel_id=1, source_target_pairs={{0,2},{1,3},{2,0},{3,1},{4,6},{5,7},{6,4},{7,5},{8,10},{9,11},{10,... | collective-permute-start | bytes 393224 | tf_op jit(solution)/shard_map/ppermute | solution.py:427
  10.6 0.0 collective-permute-start.3
  10.6 2.2 %collective-permute-start.8 = (f32[648,128]{1,0:T(8,128)S(1)}, f32[648,128]{1,0:T(8,128)S(1)}, u32[]{:S(2)}, u32[]{:S(2)}) collective-permute-start(f32[648,128]{1,0:T(8,128)S(1)} %get-tuple-element.30), channel_id=1, source_target_pairs={{0,28},{4,8},{8,4},{12,16},{16,12},{20,24},{24,20},{28,0},{1,29},{... | collective-permute-start | bytes 995336 | tf_op jit(solution)/shard_map/ppermute | solution.py:423
  12.8 0.2 collective-permute-done.1.refs_1_.refs_5_
  13.0 0.0 collective-permute-start.5
  13.0 3.8 %collective-permute-done.2.refs_2_.refs_6_ = f32[4,64,128]{2,1,0:T(8,128)S(1)} collective-permute-done((f32[4,64,128]{2,1,0:T(8,128)S(1)}, f32[4,64,128]{2,1,0:T(8,128)S(1)}, u32[]{:S(2)}, u32[]{:S(2)}) %collective-permute-start.2) | collective-permute-done | bytes 131104 | tf_op jit(solution)/shard_map/ppermute | solution.py:427
  16.9 0.0 collective-permute-start.6
  16.9 0.0 collective-permute-done.3.refs_3_.refs_7_
  16.9 0.5 %collective-permute-start.7 = (f32[4,64,128]{2,1,0:T(8,128)S(1)}, f32[4,64,128]{2,1,0:T(8,128)S(1)}, u32[]{:S(2)}, u32[]{:S(2)}) collective-permute-start(f32[4,64,128]{2,1,0:T(8,128)S(1)} %collective-permute-done.3.refs_3_.refs_7_), channel_id=1, source_target_pairs={{0,4},{4,0},{8,12},{12,8},{16,20},{20,16},{24,28},{28,24},{1,5},{5... | collective-permute-start | bytes 393224 | tf_op jit(solution)/shard_map/ppermute | solution.py:418
  17.4 0.0 copy-start.2
  18.0 0.0 collective-permute-done.5.refs_9_
  18.1 0.2 collective-permute-done.6.refs_10_
  18.2 0.2 collective-permute-done.7.refs_11_
  18.4 0.0 collective-permute-done.4.refs_8_.near
  18.4 0.0 copy-done.2
  18.4 3.1 %shard_map.47 = (bf16[2,256,640]{2,1,0:T(8,128)(2,1)S(1)}, bf16[2,256,640]{2,1,0:T(8,128)(2,1)S(1)}, bf16[2,640,256]{2,1,0:T(8,128)(2,1)S(1)}, bf16[2,640,256]{2...) custom-call(s32[1]{0:T(128)} %bitcast.even, ...), custom_call_target="tpu_custom_call" | custom-call | flops 1073741824 | bytes 4194304 | tf_op jit(solution)/shard_map/pallas_call | solution.py:369
  21.5 0.0 collective-permute-done.8.far
  21.5 12.1 %shard_map.48 = f32[2,160,640]{2,1,0:T(8,128)} custom-call(s32[1]{0:T(128)} %bitcast.even, s32[2,5]{1,0:T(2,128)S(1)} %copy-done.2, f32[1]{0:T(128)S(6)} %copy.6.fermi, s32[1]{0:T(128)} %bitcast.1.place, bf16[2,256,640]{2,1,0:T(8,128)(2,1)S(1)} %get-tuple-element.20.y_h, bf16[2,256,640]{2,1,0:T(8,128)(2,1)S(1)} %get-tuple-element.21.y_l, ...), custom_call_target="tpu_custom_call" | custom-call | flops 17179869184 | bytes 8388608 | tf_op jit(solution)/shard_map/pallas_call | solution.py:394
  (2 shorter events, 0.0 us)
Async XLA Ops:
  0.0 6.8 %collective-permute-start = (f32[2,64,128]{2,1,0:T(8,128)}, f32[2,64,128]{2,1,0:T(8,128)S(1)}, u32[]{:S(2)}, u32[]{:S(2)}) collective-permute-start(f32[2,64,128]{2,1,0:T(8,128)} %own.1), channel_id=1, source_target_pairs={{0,28},{4,8},{8,4},{12,16},{16,12},{20,24},{24,20},{28,0},{1,29},{... | collective-permute-start | bytes 196616 | tf_op jit(solution)/shard_map/ppermute | solution.py:423
  4.5 1.1 %copy-start = (f32[2,5,128,128]{3,2,1,0:T(8,128)S(1)}, f32[2,5,128,128]{3,2,1,0:T(8,128)}, u32[]{:S(2)}) copy-start(f32[2,5,128,128]{3,2,1,0:T(8,128)} %band.1) | copy-start | bytes 1966084
  5.6 0.8 %copy-start.1 = (f32[2,64,128]{2,1,0:T(8,128)S(1)}, f32[2,64,128]{2,1,0:T(8,128)}, u32[]{:S(2)}) copy-start(f32[2,64,128]{2,1,0:T(8,128)} %own.1) | copy-start | bytes 196612
  6.6 11.8 %collective-permute-start.4 = (f32[776,128]{1,0:T(8,128)S(1)}, f32[776,128]{1,0:T(8,128)S(1)}, u32[]{:S(2)}, u32[]{:S(2)}) collective-permute-start(f32[776,128]{1,0:T(8,128)S(1)} %get-tuple-element.19), channel_id=1, source_target_pairs={{0,4},{4,0},{8,12},{12,8},{16,20},{20,16},{24,28},{28,24},{1,5},{5... | collective-permute-start | bytes 1191944 | tf_op jit(solution)/shard_map/ppermute | solution.py:418
  6.8 6.3 %collective-permute-start.1 = (f32[4,64,128]{2,1,0:T(8,128)S(1)}, f32[4,64,128]{2,1,0:T(8,128)S(1)}, u32[]{:S(2)}, u32[]{:S(2)}) collective-permute-start(f32[4,64,128]{2,1,0:T(8,128)S(1)} %constant_dynamic-update-slice_fusion), channel_id=1, source_target_pairs={{0,1},{1,0},{2,3},{3,2},{4,5},{5,4},{6,7},{7,6},{8,9},{9,8},{10,11... | collective-permute-start | bytes 393224 | tf_op jit(solution)/shard_map/ppermute | solution.py:427
  9.1 7.8 %collective-permute-start.2 = (f32[4,64,128]{2,1,0:T(8,128)S(1)}, f32[4,64,128]{2,1,0:T(8,128)S(1)}, u32[]{:S(2)}, u32[]{:S(2)}) collective-permute-start(f32[4,64,128]{2,1,0:T(8,128)S(1)} %constant_dynamic-update-slice_fusion), channel_id=1, source_target_pairs={{0,2},{1,3},{2,0},{3,1},{4,6},{5,7},{6,4},{7,5},{8,10},{9,11},{10,... | collective-permute-start | bytes 393224 | tf_op jit(solution)/shard_map/ppermute | solution.py:427
  10.6 6.3 %collective-permute-start.3 = (f32[4,64,128]{2,1,0:T(8,128)S(1)}, f32[4,64,128]{2,1,0:T(8,128)S(1)}, u32[]{:S(2)}, u32[]{:S(2)}) collective-permute-start(f32[4,64,128]{2,1,0:T(8,128)S(1)} %constant_dynamic-update-slice_fusion), channel_id=1, source_target_pairs={{0,3},{1,2},{2,1},{3,0},{4,7},{5,6},{6,5},{7,4},{8,11},{9,10},{10,... | collective-permute-start | bytes 393224 | tf_op jit(solution)/shard_map/ppermute | solution.py:427
  10.6 10.9 %collective-permute-start.8 = (f32[648,128]{1,0:T(8,128)S(1)}, f32[648,128]{1,0:T(8,128)S(1)}, u32[]{:S(2)}, u32[]{:S(2)}) collective-permute-start(f32[648,128]{1,0:T(8,128)S(1)} %get-tuple-element.30), channel_id=1, source_target_pairs={{0,28},{4,8},{8,4},{12,16},{16,12},{20,24},{24,20},{28,0},{1,29},{... | collective-permute-start | bytes 995336 | tf_op jit(solution)/shard_map/ppermute | solution.py:423
  13.0 5.0 %collective-permute-start.5 = (f32[4,64,128]{2,1,0:T(8,128)S(1)}, f32[4,64,128]{2,1,0:T(8,128)S(1)}, u32[]{:S(2)}, u32[]{:S(2)}) collective-permute-start(f32[4,64,128]{2,1,0:T(8,128)S(1)} %collective-permute-done.1.refs_1_.refs_5_), channel_id=1, source_target_pairs={{0,4},{4,0},{8,12},{12,8},{16,20},{20,16},{24,28},{28,24},{1,5},{5... | collective-permute-start | bytes 393224 | tf_op jit(solution)/shard_map/ppermute | solution.py:418
  16.9 1.3 %collective-permute-start.6 = (f32[4,64,128]{2,1,0:T(8,128)S(1)}, f32[4,64,128]{2,1,0:T(8,128)S(1)}, u32[]{:S(2)}, u32[]{:S(2)}) collective-permute-start(f32[4,64,128]{2,1,0:T(8,128)S(1)} %collective-permute-done.2.refs_2_.refs_6_), channel_id=1, source_target_pairs={{0,4},{4,0},{8,12},{12,8},{16,20},{20,16},{24,28},{28,24},{1,5},{5... | collective-permute-start | bytes 393224 | tf_op jit(solution)/shard_map/ppermute | solution.py:418
  16.9 1.5 %collective-permute-start.7 = (f32[4,64,128]{2,1,0:T(8,128)S(1)}, f32[4,64,128]{2,1,0:T(8,128)S(1)}, u32[]{:S(2)}, u32[]{:S(2)}) collective-permute-start(f32[4,64,128]{2,1,0:T(8,128)S(1)} %collective-permute-done.3.refs_3_.refs_7_), channel_id=1, source_target_pairs={{0,4},{4,0},{8,12},{12,8},{16,20},{20,16},{24,28},{28,24},{1,5},{5... | collective-permute-start | bytes 393224 | tf_op jit(solution)/shard_map/ppermute | solution.py:418
  17.4 1.0 %copy-start.2 = (s32[2,5]{1,0:T(2,128)S(1)}, s32[2,5]{1,0:T(2,128)}, u32[]{:S(2)}) copy-start(s32[2,5]{1,0:T(2,128)} %mask.3) | copy-start | bytes 124

commit v5 on v4

--- a/solution.py
+++ b/solution.py
@@ -334,6 +334,17 @@
         copy.wait()
 
 
+def column_kernel(cols, reach, rep_size, even, mask, fermi, place, *refs):
+    inputs = 3 * rep_size
+    pieces, (kept, far, target) = refs[:inputs], refs[inputs : inputs + 3]
+    root, scratch = refs[inputs + 3 : inputs + 12], refs[inputs + 12 :]
+    root_kernel(cols, reach, rep_size, even, mask, *pieces, *root)
+    density_kernel(
+        cols, reach, rep_size, even, mask, fermi, place,
+        *root, kept, far, pieces[2 * rep_size], target, *scratch,
+    )
+
+
 def two_sided(one, block):
     return jnp.where(upper(block), 0.0, one.T)
 
@@ -361,42 +372,24 @@
     )(even, band, own)
 
 
-def inverse_root(even, mask, owns, fars, nears, reach):
+def density(even, mask, fermi, place, owns, fars, nears, kept, far, reach):
     rep_size = len(owns)
     cols, piece, block = owns[0].shape
     depth = piece * rep_size
     width = (2 * reach + 1) * block
-    return pl.pallas_call(
-        functools.partial(root_kernel, cols, reach, rep_size),
-        out_shape=[
-            shaped(cols, depth, width, dtype=BF16),
-            shaped(cols, depth, width, dtype=BF16),
-            shaped(cols, width, depth, dtype=BF16),
-            shaped(cols, width, depth, dtype=BF16),
-            shaped(cols, depth, width, dtype=BF16),
-            shaped(cols, depth, width, dtype=BF16),
-            shaped(cols, width, depth, dtype=BF16),
-            shaped(cols, width, depth, dtype=BF16),
-            shaped(cols, TILE, block),
-        ],
-        in_specs=[SMEM] * 2 + [VMEM] * (3 * rep_size),
-        out_specs=[VMEM] * 9,
-        compiler_params=pltpu.CompilerParams(vmem_limit_bytes=16 * 2**20),
-        cost_estimate=pl.CostEstimate(flops=2**30, bytes_accessed=4 * 2**20, transcendentals=0),
-    )(even, mask, *owns, *fars, *nears)
-
-
-def density(even, mask, fermi, place, root, kept, far, near, reach, rep_size):
-    cols, depth, width = root[0].shape
     rows = width // rep_size
-    block = width // (2 * reach + 1)
     window = (cols + 2 * reach) * block
     return pl.pallas_call(
-        functools.partial(density_kernel, cols, reach, rep_size),
+        functools.partial(column_kernel, cols, reach, rep_size),
         out_shape=shaped(cols, rows, width),
-        in_specs=[SMEM] * 4 + [VMEM] * 12,
+        in_specs=[SMEM] * 4 + [VMEM] * (3 * rep_size + 2),
         out_specs=pl.BlockSpec(memory_space=pl.ANY),
         scratch_shapes=[
+            *[pltpu.VMEM((cols, depth, width), BF16)] * 2,
+            *[pltpu.VMEM((cols, width, depth), BF16)] * 2,
+            *[pltpu.VMEM((cols, depth, width), BF16)] * 2,
+            *[pltpu.VMEM((cols, width, depth), BF16)] * 2,
+            pltpu.VMEM((cols, TILE, block), F32),
             pltpu.VMEM((window, window), F32),
             pltpu.VMEM((window, window), BF16),
             pltpu.VMEM((window, window), BF16),
@@ -411,7 +404,7 @@
         ],
         compiler_params=pltpu.CompilerParams(vmem_limit_bytes=36 * 2**20),
         cost_estimate=pl.CostEstimate(flops=2**34, bytes_accessed=8 * 2**20, transcendentals=0),
-    )(even, mask, fermi, place, *root, kept, far, near)
+    )(even, mask, fermi, place, *owns, *fars, *nears, kept, far)
 
 
 def near_swap(value):
@@ -442,8 +435,7 @@
     owns = [own] + groups[1:]
     fars = [margin_far] + groups[1:]
     nears = [near] + [near_swap(value) for value in groups[1:]]
-    root = inverse_root(even, neighbour_mask, owns, fars, nears, reach)
-    return density(even, neighbour_mask, fermi_level, place, root, kept, far, near, reach, rep_size)
+    return density(even, neighbour_mask, fermi_level, place, owns, fars, nears, kept, far, reach)
 
 
 def solution(mesh):

time: 33.8 us -> 33.4 us (0.988)
  starting transfers between devices: 11.2 us -> 8.37 us
  waiting for transfers between devices: 4.44 us -> 7.14 us
  Pallas kernels: 15.3 us -> 14.4 us
  local copies, waits for them, and re-layouts: 1.94 us -> 2.62 us
    ppermute x2, starting transfers between devices: 6.71 us -> 4.56 us  [far_swap(): lax.ppermute(value, 'cols', [(i, ((i + 1 ^ 1) - 1) % count) for i in rang...]
    ppermute x3, waiting for transfers between devices: 4.02 us -> 6.15 us  [rep_swap(): lax.ppermute(value, 'rep', [(i, i ^ step) for i in range(lax.axis_size('r...]
    pallas_call x2 -> x1, Pallas kernels: 15.2 us -> 14.2 us  [density(): pl.pallas_call(functools.partial(column_kernel, cols, reach, rep_size), o...]
    unnamed x7, local copies, waits for them, and re-layouts: 1.94 us -> 2.61 us
    ppermute x2, waiting for transfers between devices: 0.08 us -> 0.53 us  [far_swap(): lax.ppermute(value, 'cols', [(i, ((i + 1 ^ 1) - 1) % count) for i in rang...]
    ppermute x3, starting transfers between devices: 3.86 us -> 3.49 us  [rep_swap(): lax.ppermute(value, 'rep', [(i, i ^ step) for i in range(lax.axis_size('r...]
  transfers between devices with their start and end apart: 9 -> 9, of which waited for: 5 -> 6; matrix products, arithmetic and copies ran while one was open for 0% -> 0% of each run, Pallas kernels for 10% -> 0%
where the time goes in v5:
time: 33.4 us; the launch traced here: 33.2 us
  Pallas kernels  14.4 us (43%)
  starting transfers between devices  8.37 us (25%)
  waiting for transfers between devices  7.14 us (21%)
  local copies, waits for them, and re-layouts  2.62 us (8%)
  between operations  0.71 us (2%)
    pallas_call x1, Pallas kernels, density(): pl.pallas_call(functools.partial(column_kernel, cols, reach, rep_size), o...  14.2 us
    ppermute x3, waiting for transfers between devices, rep_swap(): lax.ppermute(value, 'rep', [(i, i ^ step) for i in range(lax.axis_size('r...  6.15 us
    ppermute x2, starting transfers between devices, far_swap(): lax.ppermute(value, 'cols', [(i, ((i + 1 ^ 1) - 1) % count) for i in rang...  4.56 us
    ppermute x3, starting transfers between devices, rep_swap(): lax.ppermute(value, 'rep', [(i, i ^ step) for i in range(lax.axis_size('r...  3.49 us
    unnamed x7, local copies, waits for them, and re-layouts  2.61 us
  transfers between devices with their start and end apart: 9, of which 6 were waited for; matrix products, arithmetic and copies ran while one was open for 0% of the time, Pallas kernels for 0%

profile of v5, /device:TPU:0, one launch (start us, length us, event | category | flops | bytes accessed | tf_op | source)
XLA Modules:
  0.0 33.2 jit_solution(14434588341394622493)
XLA Ops:
  0.0 4.5 %collective-permute-start = (f32[2,64,128]{2,1,0:T(8,128)}, f32[2,64,128]{2,1,0:T(8,128)S(1)}, u32[]{:S(2)}, u32[]{:S(2)}) collective-permute-start(f32[2,64,128]{2,1,0:T(8,128)} %own.1), channel_id=1, source_target_pairs={{0,28},{4,8},{8,4},{12,16},{16,12},{20,24},{24,20},{28,0},{1,29},{... | collective-permute-start | bytes 196616 | tf_op jit(solution)/shard_map/ppermute | solution.py:416
  4.5 0.0 copy-start
  4.5 1.1 %copy-done = f32[2,5,128,128]{3,2,1,0:T(8,128)S(1)} copy-done((f32[2,5,128,128]{3,2,1,0:T(8,128)S(1)}, f32[2,5,128,128]{3,2,1,0:T(8,128)}, u32[]{:S(2)}) %copy-start) | copy-done | bytes 655384
  5.6 0.0 copy-start.1
  5.6 0.8 %copy-done.1 = f32[2,64,128]{2,1,0:T(8,128)S(1)} copy-done((f32[2,64,128]{2,1,0:T(8,128)S(1)}, f32[2,64,128]{2,1,0:T(8,128)}, u32[]{:S(2)}) %copy-start.1) | copy-done | bytes 65560
  6.4 0.2 shard_map.46
  6.6 0.1 collective-permute-start.8
  6.7 0.1 collective-permute-start.4
  6.8 0.5 %collective-permute-done.refs_4_ = f32[2,64,128]{2,1,0:T(8,128)S(1)} collective-permute-done((f32[2,64,128]{2,1,0:T(8,128)}, f32[2,64,128]{2,1,0:T(8,128)S(1)}, u32[]{:S(2)}, u32[]{:S(2)}) %collective-permute-start) | collective-permute-done | bytes 65568 | tf_op jit(solution)/shard_map/ppermute | solution.py:416
  7.3 2.7 %collective-permute-start.3 = (f32[4,64,128]{2,1,0:T(8,128)S(1)}, f32[4,64,128]{2,1,0:T(8,128)S(1)}, u32[]{:S(2)}, u32[]{:S(2)}) collective-permute-start(f32[4,64,128]{2,1,0:T(8,128)S(1)} %constant_dynamic-update-slice_fusion), channel_id=1, source_target_pairs={{0,3},{1,2},{2,1},{3,0},{4,7},{5,6},{6,5},{7,4},{8,11},{9,10},{10,... | collective-permute-start | bytes 393224 | tf_op jit(solution)/shard_map/ppermute | solution.py:420
  10.0 0.5 %collective-permute-start.2 = (f32[4,64,128]{2,1,0:T(8,128)S(1)}, f32[4,64,128]{2,1,0:T(8,128)S(1)}, u32[]{:S(2)}, u32[]{:S(2)}) collective-permute-start(f32[4,64,128]{2,1,0:T(8,128)S(1)} %constant_dynamic-update-slice_fusion), channel_id=1, source_target_pairs={{0,2},{1,3},{2,0},{3,1},{4,6},{5,7},{6,4},{7,5},{8,10},{9,11},{10,... | collective-permute-start | bytes 393224 | tf_op jit(solution)/shard_map/ppermute | solution.py:420
  10.5 0.2 collective-permute-start.1
  10.8 3.2 %collective-permute-done.3.refs_3_.refs_7_ = f32[4,64,128]{2,1,0:T(8,128)S(1)} collective-permute-done((f32[4,64,128]{2,1,0:T(8,128)S(1)}, f32[4,64,128]{2,1,0:T(8,128)S(1)}, u32[]{:S(2)}, u32[]{:S(2)}) %collective-permute-start.3) | collective-permute-done | bytes 131104 | tf_op jit(solution)/shard_map/ppermute | solution.py:420
  14.0 0.0 collective-permute-start.7
  14.0 2.7 %collective-permute-done.2.refs_2_.refs_6_ = f32[4,64,128]{2,1,0:T(8,128)S(1)} collective-permute-done((f32[4,64,128]{2,1,0:T(8,128)S(1)}, f32[4,64,128]{2,1,0:T(8,128)S(1)}, u32[]{:S(2)}, u32[]{:S(2)}) %collective-permute-start.2) | collective-permute-done | bytes 131104 | tf_op jit(solution)/shard_map/ppermute | solution.py:420
  16.7 0.0 collective-permute-start.6
  16.7 0.3 collective-permute-done.1.refs_1_.refs_5_
  17.0 0.2 collective-permute-start.5
  17.8 0.0 collective-permute-done.7.refs_11_
  17.9 0.2 collective-permute-done.6.refs_10_
  18.0 0.3 collective-permute-done.5.refs_9_
  18.3 0.0 collective-permute-done.8.refs_13_
  18.3 0.0 collective-permute-done.4.refs_8_
  18.3 0.0 copy-start.2
  18.3 0.7 %copy-done.2 = s32[2,5]{1,0:T(2,128)S(1)} copy-done((s32[2,5]{1,0:T(2,128)S(1)}, s32[2,5]{1,0:T(2,128)}, u32[]{:S(2)}) %copy-start.2) | copy-done | bytes 64
  19.0 14.2 %shard_map.47 = f32[2,160,640]{2,1,0:T(8,128)} custom-call(s32[1]{0:T(128)} %bitcast.even, s32[2,5]{1,0:T(2,128)S(1)} %copy-done.2, f32[1]{0:T(128)S(6)} %copy.6.fermi, s32[1]{0:T(128)} %bitcast.1.place, f32[2,64,128]{2,1,0:T(8,128)S(1)} %get-tuple-element.9.refs_0_, f32[4,64,128]{2,1,0:T(8,128)S(1)} %collective-permute-done.1.refs_1_.refs_5_, ...), custom_call_target="tpu_custom_call" | custom-call | flops 17179869184 | bytes 8388608 | tf_op jit(solution)/shard_map/pallas_call | solution.py:382
  (2 shorter events, 0.0 us)
Async XLA Ops:
  0.0 7.3 %collective-permute-start = (f32[2,64,128]{2,1,0:T(8,128)}, f32[2,64,128]{2,1,0:T(8,128)S(1)}, u32[]{:S(2)}, u32[]{:S(2)}) collective-permute-start(f32[2,64,128]{2,1,0:T(8,128)} %own.1), channel_id=1, source_target_pairs={{0,28},{4,8},{8,4},{12,16},{16,12},{20,24},{24,20},{28,0},{1,29},{... | collective-permute-start | bytes 196616 | tf_op jit(solution)/shard_map/ppermute | solution.py:416
  4.5 1.1 %copy-start = (f32[2,5,128,128]{3,2,1,0:T(8,128)S(1)}, f32[2,5,128,128]{3,2,1,0:T(8,128)}, u32[]{:S(2)}) copy-start(f32[2,5,128,128]{3,2,1,0:T(8,128)} %band.1) | copy-start | bytes 1966084
  5.6 0.8 %copy-start.1 = (f32[2,64,128]{2,1,0:T(8,128)S(1)}, f32[2,64,128]{2,1,0:T(8,128)}, u32[]{:S(2)}) copy-start(f32[2,64,128]{2,1,0:T(8,128)} %own.1) | copy-start | bytes 196612
  6.6 11.7 %collective-permute-start.8 = (f32[648,128]{1,0:T(8,128)S(1)}, f32[648,128]{1,0:T(8,128)S(1)}, u32[]{:S(2)}, u32[]{:S(2)}) collective-permute-start(f32[648,128]{1,0:T(8,128)S(1)} %get-tuple-element.12), channel_id=1, source_target_pairs={{0,28},{4,8},{8,4},{12,16},{16,12},{20,24},{24,20},{28,0},{1,29},{... | collective-permute-start | bytes 995336 | tf_op jit(solution)/shard_map/ppermute | solution.py:416
  6.7 11.6 %collective-permute-start.4 = (f32[776,128]{1,0:T(8,128)S(1)}, f32[776,128]{1,0:T(8,128)S(1)}, u32[]{:S(2)}, u32[]{:S(2)}) collective-permute-start(f32[776,128]{1,0:T(8,128)S(1)} %get-tuple-element.10), channel_id=1, source_target_pairs={{0,4},{4,0},{8,12},{12,8},{16,20},{20,16},{24,28},{28,24},{1,5},{5... | collective-permute-start | bytes 1191944 | tf_op jit(solution)/shard_map/ppermute | solution.py:411
  7.3 6.7 %collective-permute-start.3 = (f32[4,64,128]{2,1,0:T(8,128)S(1)}, f32[4,64,128]{2,1,0:T(8,128)S(1)}, u32[]{:S(2)}, u32[]{:S(2)}) collective-permute-start(f32[4,64,128]{2,1,0:T(8,128)S(1)} %constant_dynamic-update-slice_fusion), channel_id=1, source_target_pairs={{0,3},{1,2},{2,1},{3,0},{4,7},{5,6},{6,5},{7,4},{8,11},{9,10},{10,... | collective-permute-start | bytes 393224 | tf_op jit(solution)/shard_map/ppermute | solution.py:420
  10.0 6.6 %collective-permute-start.2 = (f32[4,64,128]{2,1,0:T(8,128)S(1)}, f32[4,64,128]{2,1,0:T(8,128)S(1)}, u32[]{:S(2)}, u32[]{:S(2)}) collective-permute-start(f32[4,64,128]{2,1,0:T(8,128)S(1)} %constant_dynamic-update-slice_fusion), channel_id=1, source_target_pairs={{0,2},{1,3},{2,0},{3,1},{4,6},{5,7},{6,4},{7,5},{8,10},{9,11},{10,... | collective-permute-start | bytes 393224 | tf_op jit(solution)/shard_map/ppermute | solution.py:420
  10.5 6.4 %collective-permute-start.1 = (f32[4,64,128]{2,1,0:T(8,128)S(1)}, f32[4,64,128]{2,1,0:T(8,128)S(1)}, u32[]{:S(2)}, u32[]{:S(2)}) collective-permute-start(f32[4,64,128]{2,1,0:T(8,128)S(1)} %constant_dynamic-update-slice_fusion), channel_id=1, source_target_pairs={{0,1},{1,0},{2,3},{3,2},{4,5},{5,4},{6,7},{7,6},{8,9},{9,8},{10,11... | collective-permute-start | bytes 393224 | tf_op jit(solution)/shard_map/ppermute | solution.py:420
  14.0 3.9 %collective-permute-start.7 = (f32[4,64,128]{2,1,0:T(8,128)S(1)}, f32[4,64,128]{2,1,0:T(8,128)S(1)}, u32[]{:S(2)}, u32[]{:S(2)}) collective-permute-start(f32[4,64,128]{2,1,0:T(8,128)S(1)} %collective-permute-done.3.refs_3_.refs_7_), channel_id=1, source_target_pairs={{0,4},{4,0},{8,12},{12,8},{16,20},{20,16},{24,28},{28,24},{1,5},{5... | collective-permute-start | bytes 393224 | tf_op jit(solution)/shard_map/ppermute | solution.py:411
  16.7 1.3 %collective-permute-start.6 = (f32[4,64,128]{2,1,0:T(8,128)S(1)}, f32[4,64,128]{2,1,0:T(8,128)S(1)}, u32[]{:S(2)}, u32[]{:S(2)}) collective-permute-start(f32[4,64,128]{2,1,0:T(8,128)S(1)} %collective-permute-done.2.refs_2_.refs_6_), channel_id=1, source_target_pairs={{0,4},{4,0},{8,12},{12,8},{16,20},{20,16},{24,28},{28,24},{1,5},{5... | collective-permute-start | bytes 393224 | tf_op jit(solution)/shard_map/ppermute | solution.py:411
  17.0 1.3 %collective-permute-start.5 = (f32[4,64,128]{2,1,0:T(8,128)S(1)}, f32[4,64,128]{2,1,0:T(8,128)S(1)}, u32[]{:S(2)}, u32[]{:S(2)}) collective-permute-start(f32[4,64,128]{2,1,0:T(8,128)S(1)} %collective-permute-done.1.refs_1_.refs_5_), channel_id=1, source_target_pairs={{0,4},{4,0},{8,12},{12,8},{16,20},{20,16},{24,28},{28,24},{1,5},{5... | collective-permute-start | bytes 393224 | tf_op jit(solution)/shard_map/ppermute | solution.py:411
  18.3 0.7 %copy-start.2 = (s32[2,5]{1,0:T(2,128)S(1)}, s32[2,5]{1,0:T(2,128)}, u32[]{:S(2)}) copy-start(s32[2,5]{1,0:T(2,128)} %mask.1) | copy-start | bytes 124

commit v6 on v5

--- a/solution.py
+++ b/solution.py
@@ -50,7 +50,7 @@
     return [(i, j) for j in range(reach) for i in range(reach) if reach + j - i <= reach]
 
 
-def edge_kernel(reach, even, band, own, far, near, kept, group):
+def edge_kernel(reach, even, mask, band, own, far, near, kept, group, flags):
     block = band.shape[2]
     cross = crossing(reach)
     first = 0.5 * (band[0, reach] + band[0, reach].T)
@@ -68,6 +68,7 @@
         group[c] = own[c]
         begin = near.shape[0] + (c - cols) * piece
         near[begin : begin + piece] = own[c]
+    flags[...] = mask[...].astype(F32)
     kept[0] = first
     kept[1] = below
     kept[2] = second
@@ -114,7 +115,7 @@
     def at(index):
         return slice(index * block, (index + 1) * block)
 
-    keep = [[mask[c, a].astype(F32) for a in range(count)] for c in columns]
+    keep = [[mask[c : c + 1, a : a + 1] for a in range(count)] for c in columns]
     for w in range(window):
         x = margin(w)
         xt = x.T
@@ -176,7 +177,7 @@
     def at(index):
         return slice(index * block, (index + 1) * block)
 
-    keep = [[mask[c, a].astype(F32) for a in range(count)] for c in columns]
+    keep = [[mask[c : c + 1, a : a + 1] for a in range(count)] for c in columns]
 
     half = {}
     for side, base in ((0, 0), (1, reach + cols)):
@@ -357,19 +358,19 @@
 VMEM = pl.BlockSpec(memory_space=pltpu.VMEM)
 
 
-def edges(even, band, own):
+def edges(even, mask, band, own):
     cols, count, block, _ = band.shape
     reach = (count - 1) // 2
     cross = len(crossing(reach))
     height = (2 + cross) * block + TILE
     return pl.pallas_call(
         functools.partial(edge_kernel, reach),
-        out_shape=[shaped(height, block), shaped(height + own.shape[0] * own.shape[1], block), shaped(3 + 2 * cross, block, block), shaped(cols, *own.shape[1:])],
-        in_specs=[SMEM, VMEM, VMEM],
-        out_specs=[VMEM] * 4,
+        out_shape=[shaped(height, block), shaped(height + own.shape[0] * own.shape[1], block), shaped(3 + 2 * cross, block, block), shaped(cols, *own.shape[1:]), shaped(*mask.shape)],
+        in_specs=[SMEM, VMEM, VMEM, VMEM],
+        out_specs=[VMEM] * 5,
         compiler_params=pltpu.CompilerParams(vmem_limit_bytes=8 * 2**20),
         cost_estimate=pl.CostEstimate(flops=0, bytes_accessed=4 * 2**20, transcendentals=0),
-    )(even, band, own)
+    )(even, mask, band, own)
 
 
 def density(even, mask, fermi, place, owns, fars, nears, kept, far, reach):
@@ -382,7 +383,7 @@
     return pl.pallas_call(
         functools.partial(column_kernel, cols, reach, rep_size),
         out_shape=shaped(cols, rows, width),
-        in_specs=[SMEM] * 4 + [VMEM] * (3 * rep_size + 2),
+        in_specs=[SMEM, VMEM, SMEM, SMEM] + [VMEM] * (3 * rep_size + 2),
         out_specs=pl.BlockSpec(memory_space=pl.ANY),
         scratch_shapes=[
             *[pltpu.VMEM((cols, depth, width), BF16)] * 2,
@@ -427,7 +428,7 @@
     even = 1 - (lax.axis_index("cols").astype(jnp.int32) % 2).reshape(1)
     place = lax.axis_index("rep").astype(jnp.int32).reshape(1)
     margin_far = far_swap(margin_factors)
-    to_far, to_near, kept, own = edges(even, hamiltonian_band, margin_factors)
+    to_far, to_near, kept, own, flags = edges(even, neighbour_mask, hamiltonian_band, margin_factors)
     far = far_swap(to_far)
     near = near_swap(to_near)
     group = jnp.concatenate([own, margin_far], axis=0)
@@ -435,7 +436,7 @@
     owns = [own] + groups[1:]
     fars = [margin_far] + groups[1:]
     nears = [near] + [near_swap(value) for value in groups[1:]]
-    return density(even, neighbour_mask, fermi_level, place, owns, fars, nears, kept, far, reach)
+    return density(even, flags, fermi_level, place, owns, fars, nears, kept, far, reach)
 
 
 def solution(mesh):

time: 33.4 us -> 33 us (0.988)
  Pallas kernels: 14.4 us -> 13.9 us
    ppermute x2, waiting for transfers between devices: 0.53 us -> 0.01 us  [far_swap(): lax.ppermute(value, 'cols', [(i, ((i + 1 ^ 1) - 1) % count) for i in rang...]
    pallas_call x1, Pallas kernels: 14.2 us -> 13.8 us  [density(): pl.pallas_call(functools.partial(column_kernel, cols, reach, rep_size), o...]
    ppermute x3, waiting for transfers between devices: 6.15 us -> 6.57 us  [rep_swap(): lax.ppermute(value, 'rep', [(i, i ^ step) for i in range(lax.axis_size('r...]
  transfers between devices with their start and end apart: 9 -> 9, of which waited for: 6 -> 5; matrix products, arithmetic and copies ran while one was open for 0% -> 0% of each run, Pallas kernels for 0% -> 1%
where the time goes in v6:
time: 33 us; the launch traced here: 32.8 us
  Pallas kernels  13.9 us (42%)
  starting transfers between devices  8.46 us (26%)
  waiting for transfers between devices  7.05 us (21%)
  local copies, waits for them, and re-layouts  2.62 us (8%)
  between operations  0.72 us (2%)
    pallas_call x1, Pallas kernels, density(): pl.pallas_call(functools.partial(column_kernel, cols, reach, rep_size), o...  13.8 us
    ppermute x3, waiting for transfers between devices, rep_swap(): lax.ppermute(value, 'rep', [(i, i ^ step) for i in range(lax.axis_size('r...  6.57 us
    ppermute x2, starting transfers between devices, far_swap(): lax.ppermute(value, 'cols', [(i, ((i + 1 ^ 1) - 1) % count) for i in rang...  4.56 us
    ppermute x3, starting transfers between devices, rep_swap(): lax.ppermute(value, 'rep', [(i, i ^ step) for i in range(lax.axis_size('r...  3.56 us
    unnamed x7, local copies, waits for them, and re-layouts  2.61 us
  transfers between devices with their start and end apart: 9, of which 5 were waited for; matrix products, arithmetic and copies ran while one was open for 0% of the time, Pallas kernels for 1%

profile of v6, /device:TPU:0, one launch (start us, length us, event | category | flops | bytes accessed | tf_op | source)
XLA Modules:
  0.0 32.8 jit_solution(6024550066687631959)
XLA Ops:
  0.0 4.5 %collective-permute-start = (f32[2,64,128]{2,1,0:T(8,128)}, f32[2,64,128]{2,1,0:T(8,128)S(1)}, u32[]{:S(2)}, u32[]{:S(2)}) collective-permute-start(f32[2,64,128]{2,1,0:T(8,128)} %own.1), channel_id=1, source_target_pairs={{0,28},{4,8},{8,4},{12,16},{16,12},{20,24},{24,20},{28,0},{1,29},{... | collective-permute-start | bytes 196616 | tf_op jit(solution)/shard_map/ppermute | solution.py:417
  4.5 0.0 copy-start.2
  4.5 0.7 %copy-done.2 = s32[2,5]{1,0:T(2,128)S(1)} copy-done((s32[2,5]{1,0:T(2,128)S(1)}, s32[2,5]{1,0:T(2,128)}, u32[]{:S(2)}) %copy-start.2) | copy-done | bytes 64
  5.2 0.0 copy-start
  5.2 1.1 %copy-done = f32[2,5,128,128]{3,2,1,0:T(8,128)S(1)} copy-done((f32[2,5,128,128]{3,2,1,0:T(8,128)S(1)}, f32[2,5,128,128]{3,2,1,0:T(8,128)}, u32[]{:S(2)}) %copy-start) | copy-done | bytes 655384
  6.3 0.0 copy-start.1
  6.3 0.8 %copy-done.1 = f32[2,64,128]{2,1,0:T(8,128)S(1)} copy-done((f32[2,64,128]{2,1,0:T(8,128)S(1)}, f32[2,64,128]{2,1,0:T(8,128)}, u32[]{:S(2)}) %copy-start.1) | copy-done | bytes 65560
  7.1 0.2 shard_map.46
  7.3 0.1 collective-permute-start.8
  7.3 0.1 collective-permute-start.4
  7.4 0.0 collective-permute-done.refs_4_
  7.5 2.9 %collective-permute-start.3 = (f32[4,64,128]{2,1,0:T(8,128)S(1)}, f32[4,64,128]{2,1,0:T(8,128)S(1)}, u32[]{:S(2)}, u32[]{:S(2)}) collective-permute-start(f32[4,64,128]{2,1,0:T(8,128)S(1)} %constant_dynamic-update-slice_fusion), channel_id=1, source_target_pairs={{0,3},{1,2},{2,1},{3,0},{4,7},{5,6},{6,5},{7,4},{8,11},{9,10},{10,... | collective-permute-start | bytes 393224 | tf_op jit(solution)/shard_map/ppermute | solution.py:421
  10.4 0.5 %collective-permute-start.2 = (f32[4,64,128]{2,1,0:T(8,128)S(1)}, f32[4,64,128]{2,1,0:T(8,128)S(1)}, u32[]{:S(2)}, u32[]{:S(2)}) collective-permute-start(f32[4,64,128]{2,1,0:T(8,128)S(1)} %constant_dynamic-update-slice_fusion), channel_id=1, source_target_pairs={{0,2},{1,3},{2,0},{3,1},{4,6},{5,7},{6,4},{7,5},{8,10},{9,11},{10,... | collective-permute-start | bytes 393224 | tf_op jit(solution)/shard_map/ppermute | solution.py:421
  10.9 0.1 collective-permute-start.1
  11.0 3.6 %collective-permute-done.3.refs_3_.refs_7_ = f32[4,64,128]{2,1,0:T(8,128)S(1)} collective-permute-done((f32[4,64,128]{2,1,0:T(8,128)S(1)}, f32[4,64,128]{2,1,0:T(8,128)S(1)}, u32[]{:S(2)}, u32[]{:S(2)}) %collective-permute-start.3) | collective-permute-done | bytes 131104 | tf_op jit(solution)/shard_map/ppermute | solution.py:421
  14.7 0.0 collective-permute-start.7
  14.7 2.7 %collective-permute-done.2.refs_2_.refs_6_ = f32[4,64,128]{2,1,0:T(8,128)S(1)} collective-permute-done((f32[4,64,128]{2,1,0:T(8,128)S(1)}, f32[4,64,128]{2,1,0:T(8,128)S(1)}, u32[]{:S(2)}, u32[]{:S(2)}) %collective-permute-start.2) | collective-permute-done | bytes 131104 | tf_op jit(solution)/shard_map/ppermute | solution.py:421
  17.4 0.0 collective-permute-start.6
  17.4 0.2 collective-permute-done.1.refs_1_.refs_5_
  17.7 0.2 collective-permute-start.5
  18.5 0.0 collective-permute-done.7.refs_11_
  18.5 0.2 collective-permute-done.6.refs_10_
  18.7 0.3 collective-permute-done.5.refs_9_
  19.0 0.0 collective-permute-done.8.refs_13_
  19.0 0.0 collective-permute-done.4.refs_8_
  19.0 13.8 %shard_map.47 = f32[2,160,640]{2,1,0:T(8,128)} custom-call(s32[1]{0:T(128)} %bitcast.even, f32[2,5]{1,0:T(2,128)S(1)} %get-tuple-element.10.mask, f32[1]{0:T(128)S(6)} %copy.6.fermi, s32[1]{0:T(128)} %bitcast.1.place, f32[2,64,128]{2,1,0:T(8,128)S(1)} %get-tuple-element.11.refs_0_, f32[4,64,128]{2,1,0:T(8,128)S(1)} %collective-permute-done.1.refs_1_.refs_5_, ...), custom_call_target="tpu_custom_call" | custom-call | flops 17179869184 | bytes 8388608 | tf_op jit(solution)/shard_map/pallas_call | solution.py:383
  (2 shorter events, 0.0 us)
Async XLA Ops:
  0.0 7.4 %collective-permute-start = (f32[2,64,128]{2,1,0:T(8,128)}, f32[2,64,128]{2,1,0:T(8,128)S(1)}, u32[]{:S(2)}, u32[]{:S(2)}) collective-permute-start(f32[2,64,128]{2,1,0:T(8,128)} %own.1), channel_id=1, source_target_pairs={{0,28},{4,8},{8,4},{12,16},{16,12},{20,24},{24,20},{28,0},{1,29},{... | collective-permute-start | bytes 196616 | tf_op jit(solution)/shard_map/ppermute | solution.py:417
  4.5 0.7 %copy-start.2 = (s32[2,5]{1,0:T(2,128)S(1)}, s32[2,5]{1,0:T(2,128)}, u32[]{:S(2)}) copy-start(s32[2,5]{1,0:T(2,128)} %mask.1) | copy-start | bytes 124
  5.2 1.1 %copy-start = (f32[2,5,128,128]{3,2,1,0:T(8,128)S(1)}, f32[2,5,128,128]{3,2,1,0:T(8,128)}, u32[]{:S(2)}) copy-start(f32[2,5,128,128]{3,2,1,0:T(8,128)} %band.1) | copy-start | bytes 1966084
  6.3 0.8 %copy-start.1 = (f32[2,64,128]{2,1,0:T(8,128)S(1)}, f32[2,64,128]{2,1,0:T(8,128)}, u32[]{:S(2)}) copy-start(f32[2,64,128]{2,1,0:T(8,128)} %own.1) | copy-start | bytes 196612
  7.3 11.7 %collective-permute-start.8 = (f32[648,128]{1,0:T(8,128)S(1)}, f32[648,128]{1,0:T(8,128)S(1)}, u32[]{:S(2)}, u32[]{:S(2)}) collective-permute-start(f32[648,128]{1,0:T(8,128)S(1)} %get-tuple-element.14), channel_id=1, source_target_pairs={{0,28},{4,8},{8,4},{12,16},{16,12},{20,24},{24,20},{28,0},{1,29},{... | collective-permute-start | bytes 995336 | tf_op jit(solution)/shard_map/ppermute | solution.py:417
  7.3 11.7 %collective-permute-start.4 = (f32[776,128]{1,0:T(8,128)S(1)}, f32[776,128]{1,0:T(8,128)S(1)}, u32[]{:S(2)}, u32[]{:S(2)}) collective-permute-start(f32[776,128]{1,0:T(8,128)S(1)} %get-tuple-element.12), channel_id=1, source_target_pairs={{0,4},{4,0},{8,12},{12,8},{16,20},{20,16},{24,28},{28,24},{1,5},{5... | collective-permute-start | bytes 1191944 | tf_op jit(solution)/shard_map/ppermute | solution.py:412
  7.5 7.2 %collective-permute-start.3 = (f32[4,64,128]{2,1,0:T(8,128)S(1)}, f32[4,64,128]{2,1,0:T(8,128)S(1)}, u32[]{:S(2)}, u32[]{:S(2)}) collective-permute-start(f32[4,64,128]{2,1,0:T(8,128)S(1)} %constant_dynamic-update-slice_fusion), channel_id=1, source_target_pairs={{0,3},{1,2},{2,1},{3,0},{4,7},{5,6},{6,5},{7,4},{8,11},{9,10},{10,... | collective-permute-start | bytes 393224 | tf_op jit(solution)/shard_map/ppermute | solution.py:421
  10.4 7.0 %collective-permute-start.2 = (f32[4,64,128]{2,1,0:T(8,128)S(1)}, f32[4,64,128]{2,1,0:T(8,128)S(1)}, u32[]{:S(2)}, u32[]{:S(2)}) collective-permute-start(f32[4,64,128]{2,1,0:T(8,128)S(1)} %constant_dynamic-update-slice_fusion), channel_id=1, source_target_pairs={{0,2},{1,3},{2,0},{3,1},{4,6},{5,7},{6,4},{7,5},{8,10},{9,11},{10,... | collective-permute-start | bytes 393224 | tf_op jit(solution)/shard_map/ppermute | solution.py:421
  10.9 6.8 %collective-permute-start.1 = (f32[4,64,128]{2,1,0:T(8,128)S(1)}, f32[4,64,128]{2,1,0:T(8,128)S(1)}, u32[]{:S(2)}, u32[]{:S(2)}) collective-permute-start(f32[4,64,128]{2,1,0:T(8,128)S(1)} %constant_dynamic-update-slice_fusion), channel_id=1, source_target_pairs={{0,1},{1,0},{2,3},{3,2},{4,5},{5,4},{6,7},{7,6},{8,9},{9,8},{10,11... | collective-permute-start | bytes 393224 | tf_op jit(solution)/shard_map/ppermute | solution.py:421
  14.7 3.9 %collective-permute-start.7 = (f32[4,64,128]{2,1,0:T(8,128)S(1)}, f32[4,64,128]{2,1,0:T(8,128)S(1)}, u32[]{:S(2)}, u32[]{:S(2)}) collective-permute-start(f32[4,64,128]{2,1,0:T(8,128)S(1)} %collective-permute-done.3.refs_3_.refs_7_), channel_id=1, source_target_pairs={{0,4},{4,0},{8,12},{12,8},{16,20},{20,16},{24,28},{28,24},{1,5},{5... | collective-permute-start | bytes 393224 | tf_op jit(solution)/shard_map/ppermute | solution.py:412
  17.4 1.3 %collective-permute-start.6 = (f32[4,64,128]{2,1,0:T(8,128)S(1)}, f32[4,64,128]{2,1,0:T(8,128)S(1)}, u32[]{:S(2)}, u32[]{:S(2)}) collective-permute-start(f32[4,64,128]{2,1,0:T(8,128)S(1)} %collective-permute-done.2.refs_2_.refs_6_), channel_id=1, source_target_pairs={{0,4},{4,0},{8,12},{12,8},{16,20},{20,16},{24,28},{28,24},{1,5},{5... | collective-permute-start | bytes 393224 | tf_op jit(solution)/shard_map/ppermute | solution.py:412
  17.7 1.3 %collective-permute-start.5 = (f32[4,64,128]{2,1,0:T(8,128)S(1)}, f32[4,64,128]{2,1,0:T(8,128)S(1)}, u32[]{:S(2)}, u32[]{:S(2)}) collective-permute-start(f32[4,64,128]{2,1,0:T(8,128)S(1)} %collective-permute-done.1.refs_1_.refs_5_), channel_id=1, source_target_pairs={{0,4},{4,0},{8,12},{12,8},{16,20},{20,16},{24,28},{28,24},{1,5},{5... | collective-permute-start | bytes 393224 | tf_op jit(solution)/shard_map/ppermute | solution.py:412

commit v7 on v6

--- a/solution.py
+++ b/solution.py
@@ -119,12 +119,14 @@
     for w in range(window):
         x = margin(w)
         xt = x.T
+        x_s, xt_s = split(x), split(xt)
         for c in columns:
             a = w - c
             if 0 <= a < count:
-                m = keep[c][a]
-                y_h[c, :, at(a)], y_l[c, :, at(a)] = split(x * m)
-                yt_h[c, at(a), :], yt_l[c, at(a), :] = split(xt * m)
+                wide = jnp.broadcast_to(keep[c][a], (1, block)).astype(BF16)
+                tall = jnp.broadcast_to(keep[c][a], (1, xt.shape[1])).astype(BF16)
+                y_h[c, :, at(a)], y_l[c, :, at(a)] = x_s[0] * wide, x_s[1] * wide
+                yt_h[c, at(a), :], yt_l[c, at(a), :] = xt_s[0] * tall, xt_s[1] * tall
 
     depth = piece * rep_size
     small_eye = eye(depth, depth)

time: 33 us -> 32.9 us (level)
  no operation moved by 1% of the time
where the time goes in v7:
time: 32.9 us; the launch traced here: 32.7 us
  Pallas kernels  13.8 us (42%)
  starting transfers between devices  8.46 us (26%)
  waiting for transfers between devices  7.05 us (21%)
  local copies, waits for them, and re-layouts  2.62 us (8%)
  between operations  0.72 us (2%)
    pallas_call x1, Pallas kernels, density(): pl.pallas_call(functools.partial(column_kernel, cols, reach, rep_size), o...  13.7 us
    ppermute x3, waiting for transfers between devices, rep_swap(): lax.ppermute(value, 'rep', [(i, i ^ step) for i in range(lax.axis_size('r...  6.57 us
    ppermute x2, starting transfers between devices, far_swap(): lax.ppermute(value, 'cols', [(i, ((i + 1 ^ 1) - 1) % count) for i in rang...  4.56 us
    ppermute x3, starting transfers between devices, rep_swap(): lax.ppermute(value, 'rep', [(i, i ^ step) for i in range(lax.axis_size('r...  3.56 us
    unnamed x7, local copies, waits for them, and re-layouts  2.61 us
  transfers between devices with their start and end apart: 9, of which 5 were waited for; matrix products, arithmetic and copies ran while one was open for 0% of the time, Pallas kernels for 1%

profile of v7, /device:TPU:0, one launch (start us, length us, event | category | flops | bytes accessed | tf_op | source)
XLA Modules:
  0.0 32.7 jit_solution(16136105248364005387)
XLA Ops:
  0.0 4.5 %collective-permute-start = (f32[2,64,128]{2,1,0:T(8,128)}, f32[2,64,128]{2,1,0:T(8,128)S(1)}, u32[]{:S(2)}, u32[]{:S(2)}) collective-permute-start(f32[2,64,128]{2,1,0:T(8,128)} %own.1), channel_id=1, source_target_pairs={{0,28},{4,8},{8,4},{12,16},{16,12},{20,24},{24,20},{28,0},{1,29},{... | collective-permute-start | bytes 196616 | tf_op jit(solution)/shard_map/ppermute | solution.py:419
  4.5 0.0 copy-start.2
  4.5 0.7 %copy-done.2 = s32[2,5]{1,0:T(2,128)S(1)} copy-done((s32[2,5]{1,0:T(2,128)S(1)}, s32[2,5]{1,0:T(2,128)}, u32[]{:S(2)}) %copy-start.2) | copy-done | bytes 64
  5.2 0.0 copy-start
  5.2 1.1 %copy-done = f32[2,5,128,128]{3,2,1,0:T(8,128)S(1)} copy-done((f32[2,5,128,128]{3,2,1,0:T(8,128)S(1)}, f32[2,5,128,128]{3,2,1,0:T(8,128)}, u32[]{:S(2)}) %copy-start) | copy-done | bytes 655384
  6.3 0.0 copy-start.1
  6.3 0.8 %copy-done.1 = f32[2,64,128]{2,1,0:T(8,128)S(1)} copy-done((f32[2,64,128]{2,1,0:T(8,128)S(1)}, f32[2,64,128]{2,1,0:T(8,128)}, u32[]{:S(2)}) %copy-start.1) | copy-done | bytes 65560
  7.1 0.2 shard_map.46
  7.3 0.1 collective-permute-start.8
  7.3 0.1 collective-permute-start.4
  7.4 0.0 collective-permute-done.refs_4_
  7.5 2.9 %collective-permute-start.3 = (f32[4,64,128]{2,1,0:T(8,128)S(1)}, f32[4,64,128]{2,1,0:T(8,128)S(1)}, u32[]{:S(2)}, u32[]{:S(2)}) collective-permute-start(f32[4,64,128]{2,1,0:T(8,128)S(1)} %constant_dynamic-update-slice_fusion), channel_id=1, source_target_pairs={{0,3},{1,2},{2,1},{3,0},{4,7},{5,6},{6,5},{7,4},{8,11},{9,10},{10,... | collective-permute-start | bytes 393224 | tf_op jit(solution)/shard_map/ppermute | solution.py:423
  10.4 0.5 %collective-permute-start.2 = (f32[4,64,128]{2,1,0:T(8,128)S(1)}, f32[4,64,128]{2,1,0:T(8,128)S(1)}, u32[]{:S(2)}, u32[]{:S(2)}) collective-permute-start(f32[4,64,128]{2,1,0:T(8,128)S(1)} %constant_dynamic-update-slice_fusion), channel_id=1, source_target_pairs={{0,2},{1,3},{2,0},{3,1},{4,6},{5,7},{6,4},{7,5},{8,10},{9,11},{10,... | collective-permute-start | bytes 393224 | tf_op jit(solution)/shard_map/ppermute | solution.py:423
  10.9 0.1 collective-permute-start.1
  11.0 3.6 %collective-permute-done.3.refs_3_.refs_7_ = f32[4,64,128]{2,1,0:T(8,128)S(1)} collective-permute-done((f32[4,64,128]{2,1,0:T(8,128)S(1)}, f32[4,64,128]{2,1,0:T(8,128)S(1)}, u32[]{:S(2)}, u32[]{:S(2)}) %collective-permute-start.3) | collective-permute-done | bytes 131104 | tf_op jit(solution)/shard_map/ppermute | solution.py:423
  14.7 0.0 collective-permute-start.7
  14.7 2.7 %collective-permute-done.2.refs_2_.refs_6_ = f32[4,64,128]{2,1,0:T(8,128)S(1)} collective-permute-done((f32[4,64,128]{2,1,0:T(8,128)S(1)}, f32[4,64,128]{2,1,0:T(8,128)S(1)}, u32[]{:S(2)}, u32[]{:S(2)}) %collective-permute-start.2) | collective-permute-done | bytes 131104 | tf_op jit(solution)/shard_map/ppermute | solution.py:423
  17.4 0.0 collective-permute-start.6
  17.4 0.2 collective-permute-done.1.refs_1_.refs_5_
  17.7 0.2 collective-permute-start.5
  18.5 0.0 collective-permute-done.7.refs_11_
  18.5 0.2 collective-permute-done.6.refs_10_
  18.7 0.3 collective-permute-done.5.refs_9_
  19.0 0.0 collective-permute-done.8.refs_13_
  19.0 0.0 collective-permute-done.4.refs_8_
  19.0 13.7 %shard_map.47 = f32[2,160,640]{2,1,0:T(8,128)} custom-call(s32[1]{0:T(128)} %bitcast.even, f32[2,5]{1,0:T(2,128)S(1)} %get-tuple-element.10.mask, f32[1]{0:T(128)S(6)} %copy.6.fermi, s32[1]{0:T(128)} %bitcast.1.place, f32[2,64,128]{2,1,0:T(8,128)S(1)} %get-tuple-element.11.refs_0_, f32[4,64,128]{2,1,0:T(8,128)S(1)} %collective-permute-done.1.refs_1_.refs_5_, ...), custom_call_target="tpu_custom_call" | custom-call | flops 17179869184 | bytes 8388608 | tf_op jit(solution)/shard_map/pallas_call | solution.py:385
  (2 shorter events, 0.0 us)
Async XLA Ops:
  0.0 7.4 %collective-permute-start = (f32[2,64,128]{2,1,0:T(8,128)}, f32[2,64,128]{2,1,0:T(8,128)S(1)}, u32[]{:S(2)}, u32[]{:S(2)}) collective-permute-start(f32[2,64,128]{2,1,0:T(8,128)} %own.1), channel_id=1, source_target_pairs={{0,28},{4,8},{8,4},{12,16},{16,12},{20,24},{24,20},{28,0},{1,29},{... | collective-permute-start | bytes 196616 | tf_op jit(solution)/shard_map/ppermute | solution.py:419
  4.5 0.7 %copy-start.2 = (s32[2,5]{1,0:T(2,128)S(1)}, s32[2,5]{1,0:T(2,128)}, u32[]{:S(2)}) copy-start(s32[2,5]{1,0:T(2,128)} %mask.1) | copy-start | bytes 124
  5.2 1.1 %copy-start = (f32[2,5,128,128]{3,2,1,0:T(8,128)S(1)}, f32[2,5,128,128]{3,2,1,0:T(8,128)}, u32[]{:S(2)}) copy-start(f32[2,5,128,128]{3,2,1,0:T(8,128)} %band.1) | copy-start | bytes 1966084
  6.3 0.8 %copy-start.1 = (f32[2,64,128]{2,1,0:T(8,128)S(1)}, f32[2,64,128]{2,1,0:T(8,128)}, u32[]{:S(2)}) copy-start(f32[2,64,128]{2,1,0:T(8,128)} %own.1) | copy-start | bytes 196612
  7.3 11.7 %collective-permute-start.8 = (f32[648,128]{1,0:T(8,128)S(1)}, f32[648,128]{1,0:T(8,128)S(1)}, u32[]{:S(2)}, u32[]{:S(2)}) collective-permute-start(f32[648,128]{1,0:T(8,128)S(1)} %get-tuple-element.14), channel_id=1, source_target_pairs={{0,28},{4,8},{8,4},{12,16},{16,12},{20,24},{24,20},{28,0},{1,29},{... | collective-permute-start | bytes 995336 | tf_op jit(solution)/shard_map/ppermute | solution.py:419
  7.3 11.7 %collective-permute-start.4 = (f32[776,128]{1,0:T(8,128)S(1)}, f32[776,128]{1,0:T(8,128)S(1)}, u32[]{:S(2)}, u32[]{:S(2)}) collective-permute-start(f32[776,128]{1,0:T(8,128)S(1)} %get-tuple-element.12), channel_id=1, source_target_pairs={{0,4},{4,0},{8,12},{12,8},{16,20},{20,16},{24,28},{28,24},{1,5},{5... | collective-permute-start | bytes 1191944 | tf_op jit(solution)/shard_map/ppermute | solution.py:414
  7.5 7.2 %collective-permute-start.3 = (f32[4,64,128]{2,1,0:T(8,128)S(1)}, f32[4,64,128]{2,1,0:T(8,128)S(1)}, u32[]{:S(2)}, u32[]{:S(2)}) collective-permute-start(f32[4,64,128]{2,1,0:T(8,128)S(1)} %constant_dynamic-update-slice_fusion), channel_id=1, source_target_pairs={{0,3},{1,2},{2,1},{3,0},{4,7},{5,6},{6,5},{7,4},{8,11},{9,10},{10,... | collective-permute-start | bytes 393224 | tf_op jit(solution)/shard_map/ppermute | solution.py:423
  10.4 7.0 %collective-permute-start.2 = (f32[4,64,128]{2,1,0:T(8,128)S(1)}, f32[4,64,128]{2,1,0:T(8,128)S(1)}, u32[]{:S(2)}, u32[]{:S(2)}) collective-permute-start(f32[4,64,128]{2,1,0:T(8,128)S(1)} %constant_dynamic-update-slice_fusion), channel_id=1, source_target_pairs={{0,2},{1,3},{2,0},{3,1},{4,6},{5,7},{6,4},{7,5},{8,10},{9,11},{10,... | collective-permute-start | bytes 393224 | tf_op jit(solution)/shard_map/ppermute | solution.py:423
  10.9 6.8 %collective-permute-start.1 = (f32[4,64,128]{2,1,0:T(8,128)S(1)}, f32[4,64,128]{2,1,0:T(8,128)S(1)}, u32[]{:S(2)}, u32[]{:S(2)}) collective-permute-start(f32[4,64,128]{2,1,0:T(8,128)S(1)} %constant_dynamic-update-slice_fusion), channel_id=1, source_target_pairs={{0,1},{1,0},{2,3},{3,2},{4,5},{5,4},{6,7},{7,6},{8,9},{9,8},{10,11... | collective-permute-start | bytes 393224 | tf_op jit(solution)/shard_map/ppermute | solution.py:423
  14.7 3.9 %collective-permute-start.7 = (f32[4,64,128]{2,1,0:T(8,128)S(1)}, f32[4,64,128]{2,1,0:T(8,128)S(1)}, u32[]{:S(2)}, u32[]{:S(2)}) collective-permute-start(f32[4,64,128]{2,1,0:T(8,128)S(1)} %collective-permute-done.3.refs_3_.refs_7_), channel_id=1, source_target_pairs={{0,4},{4,0},{8,12},{12,8},{16,20},{20,16},{24,28},{28,24},{1,5},{5... | collective-permute-start | bytes 393224 | tf_op jit(solution)/shard_map/ppermute | solution.py:414
  17.4 1.3 %collective-permute-start.6 = (f32[4,64,128]{2,1,0:T(8,128)S(1)}, f32[4,64,128]{2,1,0:T(8,128)S(1)}, u32[]{:S(2)}, u32[]{:S(2)}) collective-permute-start(f32[4,64,128]{2,1,0:T(8,128)S(1)} %collective-permute-done.2.refs_2_.refs_6_), channel_id=1, source_target_pairs={{0,4},{4,0},{8,12},{12,8},{16,20},{20,16},{24,28},{28,24},{1,5},{5... | collective-permute-start | bytes 393224 | tf_op jit(solution)/shard_map/ppermute | solution.py:414
  17.7 1.3 %collective-permute-start.5 = (f32[4,64,128]{2,1,0:T(8,128)S(1)}, f32[4,64,128]{2,1,0:T(8,128)S(1)}, u32[]{:S(2)}, u32[]{:S(2)}) collective-permute-start(f32[4,64,128]{2,1,0:T(8,128)S(1)} %collective-permute-done.1.refs_1_.refs_5_), channel_id=1, source_target_pairs={{0,4},{4,0},{8,12},{12,8},{16,20},{20,16},{24,28},{28,24},{1,5},{5... | collective-permute-start | bytes 393224 | tf_op jit(solution)/shard_map/ppermute | solution.py:414
